TPU v7x, 128 devices: a whole 4x4x4 slice. The times are simulated.
128 devices in a mesh: grp: 4 (over y), patch: 32 (over z, x, core).
Axes of the slice: x: 4, y: 4, z: 4, core: 2. Of those that a mesh axis runs over, the one named last changes fastest.
Arguments:
- state: float32 [9, 60, 262144], P(None, 'grp', 'patch'), may hold values from -6 to 6
- courant_x: float32 [60, 262144], P('grp', 'patch'), may hold values from -0.45 to 0.45
- courant_y: float32 [60, 262144], P('grp', 'patch'), may hold values from -0.45 to 0.45
- surface: bfloat16 [16, 262144], P('grp', 'patch'), may hold values from -6 to 6
- w_in: bfloat16 [556, 256], replicated, may hold values from -0.25 to 0.25
- b_hidden: float32 [4, 256], replicated, may hold values from -3 to 3
- w_mid: bfloat16 [3, 256, 256], replicated, may hold values from -0.375 to 0.375
- w_out: bfloat16 [256, 540], replicated, may hold values from -0.375 to 0.375
- owner_map: int32 [2048, 1], replicated, may hold values from 0 to 31; in each aligned block of 16 rows (0 to 15, 16 to 31, ...) at most 2 rows name the same one
- neighbours: int32 [32, 4], replicated, may hold values from 0 to 31, as said below
Outputs:
- new_state: float32 [9, 60, 262144], P(None, 'grp', 'patch')
- owner_heating: float32 [256, 4096], P('grp', 'patch')
Inputs may be any that keep to these rules, and one draw needn't show every extreme that they name: owner_map[b, 0] is the owner of block b (row b % 64 of patch b // 64); within each aligned run of 16 blocks no owner is named more than 2 times, and in some run one owner exactly 2 times. The patches tile a periodic arrangement of 4 by 8: neighbours[p, 0] and neighbours[p, 1] precede and follow p along the first direction, neighbours[p, 2] and neighbours[p, 3] along the second; neighbours[neighbours[p, 0], 1] = p, neighbours[neighbours[p, 2], 3] = p, and neighbours[neighbours[p, 0], 2] = neighbours[neighbours[p, 2], 0].
All inputs are finite; a program needn't handle non-finite values.
Results may differ from a plain program's by a relative error of at most 0.0059.
The roundings to bfloat16 on the way count: a program that leaves them out, or rounds other values in their place, can miss the bound.
Values may be sent and summed in bfloat16 or wider, within the bound.
A program may use at most 640 MiB of HBM per device.

v0:
```python
import jax
import jax.numpy as jnp
from jax import lax
from jax.sharding import PartitionSpec as P

VARS = 9
LEV = 60
SURF = 16
SUBSTEPS = 3
PY = 128
PX = 64


KAPPA = 0.24
PHYS_DT = 0.05
HEAT_WEIGHT = 0.125


def strips(tracer, depth_cells):
    row_strips = jnp.stack([tracer[..., :depth_cells, :], tracer[..., -depth_cells:, :]])
    col_strips = jnp.stack(
        [
            jnp.swapaxes(tracer[..., :depth_cells], -1, -2),
            jnp.swapaxes(tracer[..., -depth_cells:], -1, -2),
        ]
    )
    return (row_strips[None], col_strips[None])


def take_patch(gathered, index):
    return jnp.take(gathered, index, axis=0)


def assemble(tracer, row_all, col_all, neighbours, beside_all, depth_cells):
    north_id, south_id, west_id, east_id = (
        beside_all[0],
        beside_all[1],
        beside_all[2],
        beside_all[3],
    )
    top_band = take_patch(row_all, north_id)[1]
    bottom_band = take_patch(row_all, south_id)[0]
    left_band = jnp.swapaxes(take_patch(col_all, west_id)[1], -1, -2)
    right_band = jnp.swapaxes(take_patch(col_all, east_id)[0], -1, -2)
    corner_nw = take_patch(row_all, neighbours[north_id, 2])[1][..., -depth_cells:]
    corner_ne = take_patch(row_all, neighbours[north_id, 3])[1][..., :depth_cells]
    corner_sw = take_patch(row_all, neighbours[south_id, 2])[0][..., -depth_cells:]
    corner_se = take_patch(row_all, neighbours[south_id, 3])[0][..., :depth_cells]
    upper_band = jnp.concatenate([corner_nw, top_band, corner_ne], axis=-1)
    middle = jnp.concatenate([left_band, tracer, right_band], axis=-1)
    lower_band = jnp.concatenate([corner_sw, bottom_band, corner_se], axis=-1)
    return jnp.concatenate([upper_band, middle, lower_band], axis=-2)


def advance(padded, along_x, along_y):
    centre = padded[..., 1:-1, 1:-1]
    northern = padded[..., :-2, 1:-1]
    southern = padded[..., 2:, 1:-1]
    western = padded[..., 1:-1, :-2]
    eastern = padded[..., 1:-1, 2:]
    return (
        centre
        - 0.5 * along_x * (southern - northern)
        - 0.5 * along_y * (eastern - western)
        + KAPPA * (northern + southern + western + eastern - 4.0 * centre)
    )


def activate(pre_act):
    return jax.nn.silu(pre_act).astype(jnp.bfloat16)


def hidden_layers(hidden, b_hidden, w_mid):
    for layer_index in range(w_mid.shape[0]):
        pre_act = (
            jnp.einsum(
                "...h,hj->...j", hidden, w_mid[layer_index], preferred_element_type=jnp.float32
            )
            + b_hidden[layer_index + 1]
        )
        hidden = activate(pre_act)
    return hidden


def on_device(
    state, courant_x, courant_y, surface, w_in, b_hidden, w_mid, w_out, owner_map, neighbours
):
    groups = lax.axis_size("grp")
    patches = lax.axis_size("patch")
    group_here = lax.axis_index("grp")
    patch_here = lax.axis_index("patch")
    level_share = LEV // groups
    surf_share = SURF // groups
    feat_share = VARS * level_share + surf_share
    quarter_rows = PX // groups
    capacity = max(2, 2 * quarter_rows // patches)
    slot_count = patches * capacity
    tracer = state.reshape(VARS, level_share, PX, PY)
    courants = jnp.concatenate(
        [courant_x.reshape(1, level_share, PX, PY), courant_y.reshape(1, level_share, PX, PY)],
        axis=0,
    )
    beside_all = jnp.take(neighbours, patch_here, axis=0)
    features = jnp.concatenate(
        [
            tracer.astype(jnp.bfloat16).reshape(VARS * level_share, PX, PY),
            surface.reshape(surf_share, PX, PY),
        ],
        axis=0,
    )
    by_quarter = features.reshape(feat_share, groups, quarter_rows, PY).transpose(1, 2, 0, 3)
    owners_all = owner_map.reshape(patches, groups, quarter_rows)
    owners_here = jnp.take(owners_all, patch_here, axis=0)
    matches = (owners_here[..., None] == jnp.arange(patches, dtype=jnp.int32)).astype(jnp.int32)
    slot_rank = jnp.sum((jnp.cumsum(matches, axis=1) - matches) * matches, axis=2)
    slot_index = owners_here * capacity + slot_rank
    selector = (
        slot_index[:, None, :] == jnp.arange(slot_count, dtype=jnp.int32)[None, :, None]
    ).astype(jnp.bfloat16)
    selector_here = jnp.take(selector, group_here, axis=0)
    state_part = (
        w_in[: VARS * LEV]
        .reshape(VARS, groups, level_share, -1)
        .transpose(1, 0, 2, 3)
        .reshape(groups, VARS * level_share, -1)
    )
    w_local = jnp.concatenate(
        [state_part, w_in[VARS * LEV :].reshape(groups, surf_share, -1)], axis=1
    )
    w_split = w_out.reshape(-1, VARS, groups, level_share)
    regrouped = lax.all_to_all(by_quarter, "grp", split_axis=0, concat_axis=0, tiled=True)
    pre_act = (
        jnp.einsum("gbfc,gfh->bch", regrouped, w_local, preferred_element_type=jnp.float32)
        + b_hidden[0]
    )
    hidden = hidden_layers(activate(pre_act), b_hidden, w_mid)
    tendency = jnp.einsum(
        "bch,hvgl->bvglc", hidden, w_split, preferred_element_type=jnp.float32
    ).astype(jnp.bfloat16)
    heating = HEAT_WEIGHT * jnp.sum(tendency[:, 0].astype(jnp.float32), axis=(1, 2))
    packed = jnp.dot(
        selector_here.astype(jnp.float32), heating, precision=lax.Precision.HIGHEST
    ).reshape(patches, capacity, PY)
    owner_heating = lax.all_to_all(
        packed, "patch", split_axis=0, concat_axis=0, tiled=True
    ).reshape(slot_count, PY)
    arrived = lax.all_to_all(tendency, "grp", split_axis=2, concat_axis=0, tiled=True)
    tendency_here = arrived.reshape(PX, VARS, level_share, PY).transpose(1, 2, 0, 3)
    advected = tracer
    for section_index in range(SUBSTEPS):
        row_edges, col_edges = strips(advected, 1)
        row_edges, col_edges = (
            lax.all_gather(row_edges.astype(jnp.bfloat16), "patch", axis=0, tiled=True).astype(
                row_edges.dtype
            ),
            lax.all_gather(col_edges.astype(jnp.bfloat16), "patch", axis=0, tiled=True).astype(
                col_edges.dtype
            ),
        )
        padded = assemble(advected, row_edges, col_edges, neighbours, beside_all, 1)
        advected = advance(padded, courants[0:1], courants[1:2])
    new_state = advected + PHYS_DT * tendency_here.astype(jnp.float32)
    return (new_state.reshape(VARS, level_share, PX * PY), owner_heating)


def solution(mesh):
    placed = (
        P(None, "grp", "patch"),
        P("grp", "patch"),
        P("grp", "patch"),
        P("grp", "patch"),
        P(),
        P(),
        P(),
        P(),
        P(),
        P(),
    )
    return jax.shard_map(
        on_device,
        mesh=mesh,
        in_specs=placed,
        out_specs=(P(None, "grp", "patch"), P("grp", "patch")),
        check_vma=False,
    )
```

profile of v0, /device:TPU:0, one launch (start us, length us, event | category | flops | bytes accessed | tf_op | source)
XLA Modules:
  0.0 360.9 jit_solution(12292110008784693230)
XLA Ops:
  7.2 5.9 %reshape.180 = f32[9,15,64,128]{3,2,1,0:T(8,128)} reshape(f32[9,15,8192]{2,1,0:T(8,128)} %param.14) | data formatting | bytes 8847360 | tf_op jit(solution)/shard_map/reshape | solution.py:98
  16.0 3.0 slice_reduce_fusion.5
  38.4 28.3 %all-gather.13.cloned.1.call-done = bf16[64,9,15,1,64]{4,2,3,1,0:T(8,128)(2,1)} async-done(((bf16[2,9,15,1,64]{4,2,3,1,0:T(8,128)(2,1)}), bf16[64,9,15,1,64]{4,2,3,1,0:T(8,128)(2,1)}) %all-gather.13.cloned.1.call-update) | async-done | bytes 1105936 | tf_op jit(solution)/shard_map/all_gather | solution.py:156
  72.1 3.0 copy.112
  75.1 37.4 %all-gather.15.cloned.1.call-done = bf16[64,9,15,1,128]{4,2,3,1,0:T(8,128)(2,1)} async-done(((bf16[2,9,15,1,128]{4,2,3,1,0:T(8,128)(2,1)}), bf16[64,9,15,1,128]{4,2,3,1,0:T(8,128)(2,1)}) %all-gather.15.cloned.1.call-update) | async-done | bytes 2211856 | tf_op jit(solution)/shard_map/all_gather | solution.py:153
  118.6 8.4 %fusion.54 = (bf16[9,15,64,128]{3,2,1,0:T(8,128)(2,1)S(1)}, f32[9,15,64,128]{3,2,1,0:T(8,128)}) fusion(f32[9,15,64,128]{3,2,1,0:T(8,128)S(1)} %bitcast.231, f32[9,15,64,1]{3,2,1,0:T(8,128)S(1)} %copy-done.3, f32[9,15,64,1]{3,2,1,0:T(8,128)S(1)} %copy-done.5, f32[15,64,128]{2,1,0:T(8,128)S(1)} %slice.437, f32[9,15,1,1]{3,2,1,0:T(1,128)S(1)} %bitcast.250, ...), kind=kLoop, calls=%fused_computation.172 | loop fusion | flops 28753920 | bytes 12251760 | tf_op jit(solution)/shard_map/convert.24
  126.9 3.0 slice_reduce_fusion.3
  134.3 3.1 convert_element_type.149
  141.0 4.5 %all-to-all-start = ((bf16[4,16,139,128]{3,1,2,0:T(8,128)(2,1)}), bf16[4,16,139,128]{3,1,2,0:T(8,128)(2,1)}, u32[]{:S(2)}, u32[]{:S(2)}) async-start(bf16[4,16,139,128]{3,1,2,0:T(8,128)(2,1)} %copy.135), calls=%async_computation | async-start | bytes 4554752 | tf_op jit(solution)/shard_map/all_to_all | solution.py:131
  145.5 28.7 %all-gather.17.cloned.1.call-done = bf16[64,9,15,1,64]{4,2,3,1,0:T(8,128)(2,1)} async-done(((bf16[2,9,15,1,64]{4,2,3,1,0:T(8,128)(2,1)}), bf16[64,9,15,1,64]{4,2,3,1,0:T(8,128)(2,1)}) %all-gather.17.cloned.1.call-update) | async-done | bytes 1105936 | tf_op jit(solution)/shard_map/all_gather | solution.py:156
  179.8 3.0 copy.121
  182.8 37.3 %all-gather.19.cloned.1.call-done = bf16[64,9,15,1,128]{4,2,3,1,0:T(8,128)(2,1)} async-done(((bf16[2,9,15,1,128]{4,2,3,1,0:T(8,128)(2,1)}), bf16[64,9,15,1,128]{4,2,3,1,0:T(8,128)(2,1)}) %all-gather.19.cloned.1.call-update) | async-done | bytes 2211856 | tf_op jit(solution)/shard_map/all_gather | solution.py:153
  226.1 8.4 %fusion.53 = (bf16[9,15,64,128]{3,2,1,0:T(8,128)(2,1)S(1)}, f32[9,15,64,128]{3,2,1,0:T(8,128)}) fusion(f32[9,15,64,128]{3,2,1,0:T(8,128)S(1)} %bitcast.235, f32[9,15,64,1]{3,2,1,0:T(8,128)S(1)} %copy-done.2, f32[9,15,64,1]{3,2,1,0:T(8,128)S(1)} %copy-done.4, f32[15,64,128]{2,1,0:T(8,128)S(1)} %slice.437, f32[9,15,1,1]{3,2,1,0:T(1,128)S(1)} %bitcast.249, ...), kind=kLoop, calls=%fused_computation.171 | loop fusion | flops 28753920 | bytes 12251760 | tf_op jit(solution)/shard_map/convert.12
  234.5 3.0 slice_reduce_fusion.1
  247.9 4.7 %multiply_convert_fusion.2 = bf16[16,128,256]{2,1,0:T(8,128)(2,1)} fusion(f32[256]{0:T(256)S(1)} %bitcast.269, bf16[4,16,139,128]{3,1,2,0:T(8,128)(2,1)} %all-to-all-done, f32[256]{0:T(256)S(1)} %bitcast.270, bf16[4,4,256]{2,1,0:T(4,128)(2,1)S(1)} %reshape.183, bf16[4,135,256]{2,1,0:T(8,128)(2,1)} %copy.137, bf16[3,256,256]{2,1,0:T(8,128)(2,1)} %param.20), kind=kOutput, calls=%fused_computation.53 | convolution fusion | flops 858304512 | bytes 3745792 | tf_op jit(solution)/shard_map/...h,hj->...j/dot_general | solution.py:76
  259.8 5.2 %all-to-all-start.2 = ((f32[32,2,128]{2,1,0:T(2,128)}), f32[32,2,128]{2,1,0:T(2,128)S(1)}, u32[]{:S(2)}, u32[]{:S(2)}) async-start(f32[32,2,128]{2,1,0:T(2,128)} %bitcast.99), calls=%async_computation.2 | async-start | bytes 65536 | tf_op jit(solution)/shard_map/all_to_all | solution.py:144
  265.1 3.9 %copy.139 = bf16[16,9,4,15,128]{4,0,3,1,2:T(8,128)(2,1)} copy(bf16[16,9,4,15,128]{4,3,2,1,0:T(8,128)(2,1)S(1)} %convert_bitcast_fusion) | data formatting | bytes 4423680 | tf_op jit(solution)/shard_map/convert_element_type | solution.py:139
  269.0 3.5 all-to-all-done.2
  272.5 4.5 %all-to-all-start.1 = ((bf16[16,9,4,15,128]{4,0,3,1,2:T(8,128)(2,1)}), bf16[16,9,4,15,128]{4,0,3,1,2:T(8,128)(2,1)S(1)}, u32[]{:S(2)}, u32[]{:S(2)}) async-start(bf16[16,9,4,15,128]{4,0,3,1,2:T(8,128)(2,1)} %copy.139), calls=%async_computation.1 | async-start | bytes 4423680 | tf_op jit(solution)/shard_map/all_to_all | solution.py:147
  277.0 27.8 %all-to-all-done.1 = bf16[16,9,4,15,128]{4,0,3,1,2:T(8,128)(2,1)S(1)} async-done(((bf16[16,9,4,15,128]{4,0,3,1,2:T(8,128)(2,1)}), bf16[16,9,4,15,128]{4,0,3,1,2:T(8,128)(2,1)S(1)}, u32[]{:S(2)}, u32[]{:S(2)}) %all-to-all-start.1) | async-done | bytes 2211872 | tf_op jit(solution)/shard_map/all_to_all | solution.py:147
  313.1 3.0 copy.129
  316.1 11.5 %all-gather.23.cloned.1.call-done = bf16[64,9,15,1,128]{4,2,3,1,0:T(8,128)(2,1)} async-done(((bf16[2,9,15,1,128]{4,2,3,1,0:T(8,128)(2,1)}), bf16[64,9,15,1,128]{4,2,3,1,0:T(8,128)(2,1)}) %all-gather.23.cloned.1.call-update) | async-done | bytes 2211856 | tf_op jit(solution)/shard_map/all_gather | solution.py:153
  333.7 13.9 %bitcast_add_fusion = f32[9,15,64,128]{3,2,1,0:T(8,128)} fusion(f32[16,9,4,15,128]{4,0,2,3,1:T(8,128)S(1)} %bitcast.233, f32[9,15,64,128]{3,2,1,0:T(8,128)} %get-tuple-element.66, f32[9,15,64,1]{3,2,1,0:T(8,128)S(1)} %copy-done, f32[9,15,64,1]{3,2,1,0:T(8,128)S(1)} %copy-done.1, f32[9,15,1,1]{3,2,1,0:T(1,128)S(1)} %bitcast.251, ...), kind=kLoop, calls=%fused_computation.36 | loop fusion | flops 28753920 | bytes 14463600 | tf_op jit(solution)/shard_map/add | solution.py:162
  347.6 5.6 %reshape.185 = f32[9,15,8192]{2,1,0:T(8,128)} reshape(f32[9,15,64,128]{3,2,1,0:T(8,128)} %bitcast_add_fusion) | data formatting | bytes 8847360 | tf_op jit(solution)/shard_map/reshape | solution.py:163
  (157 shorter events, 69.7 us)
Async XLA Ops:
  7.2 59.4 %all-gather.13.cloned.1.call-start = ((), (), s32[]{:S(2)}) async-start(), calls=%async_computation.3 | async-start | bytes 2433024 | tf_op jit(solution)/shard_map/all_gather | solution.py:156
  13.1 7.9 %copy-start.10 = (s32[32,4]{0,1:T(4,128)S(1)}, s32[32,4]{0,1:T(4,128)}, u32[]{:S(2)}) copy-start(s32[32,4]{0,1:T(4,128)} %param.23) | copy-start | bytes 1540
  15.9 22.0 %copy-start.6 = (f32[15,8192]{1,0:T(8,128)S(1)}, f32[15,8192]{1,0:T(8,128)}, u32[]{:S(2)}) copy-start(f32[15,8192]{1,0:T(8,128)} %param.15) | copy-start | bytes 1474564
  16.0 22.2 %copy-start.7 = (f32[15,8192]{1,0:T(8,128)S(1)}, f32[15,8192]{1,0:T(8,128)}, u32[]{:S(2)}) copy-start(f32[15,8192]{1,0:T(8,128)} %param.16) | copy-start | bytes 1474564
  19.6 92.9 %all-gather.15.cloned.1.call-start = ((), (), s32[]{:S(2)}) async-start(), calls=%async_computation.4 | async-start | bytes 2433024 | tf_op jit(solution)/shard_map/all_gather | solution.py:153
  20.5 153.8 %all-gather.17.cloned.1.call-start = ((), (), s32[]{:S(2)}) async-start(), calls=%async_computation.5 | async-start | bytes 2433024 | tf_op jit(solution)/shard_map/all_gather | solution.py:156
  112.5 5.9 %copy-start.5 = (f32[9,15,64,1]{3,2,1,0:T(8,128)S(1)}, f32[9,15,64,1]{3,2,1,0:T(8,128)}, u32[]{:S(2)}) copy-start(f32[9,15,64,1]{3,2,1,0:T(8,128)} %copy.112) | copy-start | bytes 103684
  114.9 3.5 slice-start
  114.9 3.6 %copy-start.3 = (f32[9,15,64,1]{3,2,1,0:T(8,128)S(1)}, f32[9,15,64,1]{3,2,1,0:T(8,128)}, u32[]{:S(2)}) copy-start(f32[9,15,64,1]{3,2,1,0:T(8,128)} %copy.111) | copy-start | bytes 103684
  129.9 4.4 %copy-start.8 = (bf16[4,8192]{1,0:T(4,128)(2,1)S(1)}, bf16[4,8192]{1,0:T(4,128)(2,1)}, u32[]{:S(2)}) copy-start(bf16[4,8192]{1,0:T(4,128)(2,1)} %param.17) | copy-start | bytes 196612
  130.6 89.5 %all-gather.19.cloned.1.call-start = ((), (), s32[]{:S(2)}) async-start(), calls=%async_computation.6 | async-start | bytes 2433024 | tf_op jit(solution)/shard_map/all_gather | solution.py:153
  141.0 107.0 %all-to-all-start = ((bf16[4,16,139,128]{3,1,2,0:T(8,128)(2,1)}), bf16[4,16,139,128]{3,1,2,0:T(8,128)(2,1)}, u32[]{:S(2)}, u32[]{:S(2)}) async-start(bf16[4,16,139,128]{3,1,2,0:T(8,128)(2,1)} %copy.135), calls=%async_computation | async-start | bytes 4554752 | tf_op jit(solution)/shard_map/all_to_all | solution.py:131
  145.5 162.1 %all-gather.21.cloned.1.call-start = ((), (), s32[]{:S(2)}) async-start(), calls=%async_computation.7 | async-start | bytes 2433024 | tf_op jit(solution)/shard_map/all_gather | solution.py:156
  220.1 5.9 %copy-start.4 = (f32[9,15,64,1]{3,2,1,0:T(8,128)S(1)}, f32[9,15,64,1]{3,2,1,0:T(8,128)}, u32[]{:S(2)}) copy-start(f32[9,15,64,1]{3,2,1,0:T(8,128)} %copy.121) | copy-start | bytes 103684
  222.5 3.5 slice-start.4
  222.5 3.6 %copy-start.2 = (f32[9,15,64,1]{3,2,1,0:T(8,128)S(1)}, f32[9,15,64,1]{3,2,1,0:T(8,128)}, u32[]{:S(2)}) copy-start(f32[9,15,64,1]{3,2,1,0:T(8,128)} %copy.120) | copy-start | bytes 103684
  234.5 6.8 %copy-start.9 = (s32[2048,1]{0,1:T(1,128)S(1)}, s32[2048,1]{0,1:T(1,128)}, u32[]{:S(2)}) copy-start(s32[2048,1]{0,1:T(1,128)} %param.22) | copy-start | bytes 24580
  234.5 13.4 %copy-start.11 = (f32[4,256]{1,0:T(4,128)S(1)}, f32[4,256]{1,0:T(4,128)}, u32[]{:S(2)}) copy-start(f32[4,256]{1,0:T(4,128)} %param.19) | copy-start | bytes 12292
  238.2 89.5 %all-gather.23.cloned.1.call-start = ((), (), s32[]{:S(2)}) async-start(), calls=%async_computation.8 | async-start | bytes 2433024 | tf_op jit(solution)/shard_map/all_gather | solution.py:153
  259.8 12.7 %all-to-all-start.2 = ((f32[32,2,128]{2,1,0:T(2,128)}), f32[32,2,128]{2,1,0:T(2,128)S(1)}, u32[]{:S(2)}, u32[]{:S(2)}) async-start(f32[32,2,128]{2,1,0:T(2,128)} %bitcast.99), calls=%async_computation.2 | async-start | bytes 65536 | tf_op jit(solution)/shard_map/all_to_all | solution.py:144
  272.5 32.4 %all-to-all-start.1 = ((bf16[16,9,4,15,128]{4,0,3,1,2:T(8,128)(2,1)}), bf16[16,9,4,15,128]{4,0,3,1,2:T(8,128)(2,1)S(1)}, u32[]{:S(2)}, u32[]{:S(2)}) async-start(bf16[16,9,4,15,128]{4,0,3,1,2:T(8,128)(2,1)} %copy.139), calls=%async_computation.1 | async-start | bytes 4423680 | tf_op jit(solution)/shard_map/all_to_all | solution.py:147
  327.7 5.9 %copy-start.1 = (f32[9,15,64,1]{3,2,1,0:T(8,128)S(1)}, f32[9,15,64,1]{3,2,1,0:T(8,128)}, u32[]{:S(2)}) copy-start(f32[9,15,64,1]{3,2,1,0:T(8,128)} %copy.129) | copy-start | bytes 103684
  330.1 3.5 slice-start.2
  330.1 3.6 %copy-start = (f32[9,15,64,1]{3,2,1,0:T(8,128)S(1)}, f32[9,15,64,1]{3,2,1,0:T(8,128)}, u32[]{:S(2)}) copy-start(f32[9,15,64,1]{3,2,1,0:T(8,128)} %copy.130) | copy-start | bytes 103684
  (3 other events, 10.5 us)
Sparse Core Ops, SparseCore 0:
  19.7 46.8 all-gather.12
  68.9 43.5 all-gather.14
  130.7 43.5 all-gather.16
  176.4 43.6 all-gather.18
  238.3 43.5 all-gather.20
  284.0 43.5 all-gather.22
where the time goes:
time: 367 us; the launch traced here: 361 us
  waiting for transfers between devices  175 us (48%)
  local copies, waits for them, and re-layouts  68.4 us (19%)
  other arithmetic  60.8 us (17%)
  between operations  30.8 us (8%)
  starting transfers between devices  15.3 us (4%)
  matrix products  11 us (3%)
    all_gather x3, waiting for transfers between devices, on_device(): lax.all_gather(row_edges.astype(jnp.bfloat16), 'patch', axis=0, tiled=True)  86.3 us
    all_gather x3, waiting for transfers between devices, on_device(): lax.all_gather(col_edges.astype(jnp.bfloat16), 'patch', axis=0, tiled=True)  57 us
    all_to_all x1, waiting for transfers between devices, on_device(): lax.all_to_all(tendency, 'grp', split_axis=2, concat_axis=0, tiled=True)  27.8 us
    another operation x3, other arithmetic  19.5 us
    add x1, other arithmetic, on_device(): new_state = advected + PHYS_DT * tendency_here.astype(jnp.float32)  13.9 us
    another operation x6, local copies, waits for them, and re-layouts, assemble(): right_band = jnp.swapaxes(take_patch(col_all, east_id)[0], -1, -2)  9.03 us
    another operation x6, local copies, waits for them, and re-layouts, assemble(): left_band = jnp.swapaxes(take_patch(col_all, west_id)[1], -1, -2)  9 us
    slice x3, local copies, waits for them, and re-layouts, strips(): tracer[..., :depth_cells]  8.89 us
  transfers between devices with their start and end apart: 9, of which 7 were waited for; matrix products, arithmetic and copies ran while one was open for 23% of the time, Pallas kernels for 0%

commit v1 on v0

v1 whole, which is shorter than its diff:
```python
import jax
import jax.numpy as jnp
from jax import lax
from jax.experimental import pallas as pl
from jax.experimental.pallas import tpu as pltpu
from jax.sharding import PartitionSpec as P

MESH = pl.DeviceIdType.MESH
F32 = jnp.float32
BF16 = jnp.bfloat16

VARS = 9
LEV = 60
SHARE = 15
SURF = 16
SSHARE = 4
HID = 256
MIDS = 3
PX = 64
LANES = 128
COLS = PX * LANES
QUARTER = COLS // 4
ROWS = VARS * 16
FEAT = 556
OUTF = 540
CHUNKS = 4
WIDE = QUARTER // CHUNKS
HALF = WIDE // 2
ROUNDS = 3
SPLIT = 5
GROUP_VARS = ((0, SPLIT), (SPLIT, VARS))
GROUP_ROWS = (SPLIT * 16, (VARS - SPLIT) * 16)

KAPPA = 0.24
PHYS_DT = 0.05
HEAT_WEIGHT = 0.125


def kernel(
    owner_ref, nbr_ref, state, courx, coury, surf, w_in, b_hid, w_mid, w_out,
    out, heat_out,
    S, T1, T2, CX, CY, F, X, FP, FM, TO, TR, OP, OM,
    W1, WM, W2, BB, CB, HT, PK, PR,
    GA0, GB0, SA0, SB0, RA0, RB0, GA1, GB1, SA1, SB1, RA1, RB1, GA2, GB2, SA2, SB2, RA2, RB2,
    load_sem, cour_sem, store_sem,
    in_s, in_r, fw_s, fw_r, out_s, out_r, of_s, of_r,
    p1_s, p1_r, p2_s, p2_r, p3_s, p3_r, ht_s, ht_r,
):
    g = lax.axis_index("grp")
    p = lax.axis_index("patch")
    zi, xi, ci = p // 8, (p // 2) % 4, p % 2
    gp, gm, go = (g + 1) % 4, (g + 3) % 4, (g + 2) % 4

    def rcopy(src, dst, ss, rs, dev):
        return pltpu.make_async_remote_copy(
            src_ref=src, dst_ref=dst, send_sem=ss, recv_sem=rs, device_id=dev, device_id_type=MESH
        )

    def col0(q, c):
        return pl.multiple_of(q * QUARTER + c * WIDE, LANES)

    order = (go, gp, gm, g)

    def load(c, i):
        off = col0(order[i], c)
        return pltpu.make_async_copy(
            state.at[:, :, pl.ds(off, WIDE)],
            S.at[:, :, pl.ds(pl.multiple_of(off + LANES, LANES), WIDE)],
            load_sem.at[c, i],
        )

    for c in range(CHUNKS):
        for i in range(4):
            load(c, i).start()
    cour = (
        pltpu.make_async_copy(courx, CX, cour_sem.at[0]),
        pltpu.make_async_copy(coury, CY, cour_sem.at[1]),
    )
    for copy in cour:
        copy.start()

    barrier = pltpu.get_barrier_semaphore()
    for other in (gp, gm, go):
        pl.semaphore_signal(barrier, inc=1, device_id=(other, p), device_id_type=MESH)

    def greet(d, carry):
        pl.semaphore_signal(barrier, inc=1, device_id=(g, (p + d) % 32), device_id_type=MESH)
        return carry

    lax.fori_loop(1, 32, greet, 0)
    pl.semaphore_wait(barrier, 34)

    def cast(q, c, own):
        off = col0(q, c)
        here = pl.multiple_of(off + LANES, LANES)
        for v in range(VARS):
            value = S[v, :, pl.ds(here, WIDE)]
            if v < SSHARE:
                extra = surf[v : v + 1, pl.ds(off, WIDE)].astype(F32)
            else:
                extra = jnp.zeros((1, WIDE), F32)
            value = jnp.concatenate([value, extra], axis=0).astype(BF16)
            F[q, pl.ds(v * 16, 16), pl.ds(c * WIDE, WIDE)] = value
            if own:
                X[pl.ds(pl.multiple_of(g * ROWS + v * 16, 16), 16), pl.ds(c * WIDE, WIDE)] = value

    mine = pl.ds(pl.multiple_of(g * ROWS, 16), ROWS)
    prev_rows = pl.ds(pl.multiple_of(gm * ROWS, 16), ROWS)
    next_rows = pl.ds(pl.multiple_of(gp * ROWS, 16), ROWS)
    far_rows = pl.ds(pl.multiple_of(go * ROWS, 16), ROWS)

    def in_copies(c):
        lo, hi, whole = pl.ds(c * WIDE, HALF), pl.ds(c * WIDE + HALF, HALF), pl.ds(c * WIDE, WIDE)
        return (
            rcopy(F.at[go, :, lo], FP.at[c], in_s.at[c, 0], in_r.at[c, 0], (gp, p)),
            rcopy(F.at[go, :, hi], FM.at[c], in_s.at[c, 1], in_r.at[c, 1], (gm, p)),
            rcopy(F.at[gp, :, whole], X.at[mine, whole], in_s.at[c, 2], in_r.at[c, 2], (gp, p)),
            rcopy(F.at[gm, :, whole], X.at[mine, whole], in_s.at[c, 3], in_r.at[c, 3], (gm, p)),
        )

    def in_forwards(c):
        lo, hi = pl.ds(c * WIDE, HALF), pl.ds(c * WIDE + HALF, HALF)
        return (
            rcopy(FP.at[c], X.at[prev_rows, lo], fw_s.at[c, 0], fw_r.at[c, 0], (gp, p)),
            rcopy(FM.at[c], X.at[next_rows, hi], fw_s.at[c, 1], fw_r.at[c, 1], (gm, p)),
        )

    def out_copies(c):
        lo, hi, whole = pl.ds(c * WIDE, HALF), pl.ds(c * WIDE + HALF, HALF), pl.ds(c * WIDE, WIDE)
        return (
            rcopy(TO.at[far_rows, lo], OP.at[c], out_s.at[c, 0], out_r.at[c, 0], (gp, p)),
            rcopy(TO.at[far_rows, hi], OM.at[c], out_s.at[c, 1], out_r.at[c, 1], (gm, p)),
            rcopy(TO.at[next_rows, whole], TR.at[g, :, whole], out_s.at[c, 2], out_r.at[c, 2], (gp, p)),
            rcopy(TO.at[prev_rows, whole], TR.at[g, :, whole], out_s.at[c, 3], out_r.at[c, 3], (gm, p)),
        )

    def out_forwards(c):
        lo, hi = pl.ds(c * WIDE, HALF), pl.ds(c * WIDE + HALF, HALF)
        return (
            rcopy(OP.at[c], TR.at[gm, :, lo], of_s.at[c, 0], of_r.at[c, 0], (gp, p)),
            rcopy(OM.at[c], TR.at[gp, :, hi], of_s.at[c, 1], of_r.at[c, 1], (gm, p)),
        )

    for c in range(CHUNKS):
        for i in range(3):
            load(c, i).wait()
            cast(order[i], c, False)
            copies = in_copies(c)
            if i == 0:
                copies[0].start()
                copies[1].start()
            else:
                copies[i + 1].start()
    for c in range(CHUNKS):
        load(c, 3).wait()
        cast(g, c, True)

    halo = (
        ((GA0, SA0, RA0), (GB0, SB0, RB0)),
        ((GA1, SA1, RA1), (GB1, SB1, RB1)),
        ((GA2, SA2, RA2), (GB2, SB2, RB2)),
    )
    first = (xi, zi)
    second = (zi, xi)
    even = lax.broadcasted_iota(jnp.int32, (16, LANES), 1) % 2 == 0

    def patch_of(k, one, two, core):
        return two * 8 + one * 2 + core if k == 0 else one * 8 + two * 2 + core

    def spots(k, n):
        z, x, core = n // 8, (n // 2) % 4, n % 2
        return (x, z, core) if k == 0 else (z, x, core)

    def p1_copies(r, k):
        G = halo[r][k][0]
        return [
            rcopy(
                G.at[ci, first[k]], G.at[ci, first[k]], p1_s.at[r, k, d - 1], p1_r.at[r, k, d - 1],
                (g, patch_of(k, (first[k] + d) % 4, second[k], ci)),
            )
            for d in (2, 1, 3)
        ]

    def p2_copy(r, k):
        G = halo[r][k][0]
        return rcopy(
            G.at[ci], G.at[ci], p2_s.at[r, k], p2_r.at[r, k],
            (g, patch_of(k, first[k], second[k], 1 - ci)),
        )

    def p3_copy(r, k, d):
        _, Sd, R = halo[r][k]
        return rcopy(
            Sd.at[d], R.at[second[k]], p3_s.at[r, k, d - 1], p3_r.at[r, k, d - 1],
            (g, patch_of(k, first[k], (second[k] + d) % 4, ci)),
        )

    def put_edge(r, strip, v, value):
        k = 0 if v < SPLIT else 1
        G = halo[r][k][0]
        G[ci, first[k], strip, pl.ds((v - GROUP_VARS[k][0]) * 16, 16), :] = jnp.concatenate(
            [value, jnp.zeros((1, LANES), F32)], axis=0
        ).astype(BF16)

    def start_p1(r):
        for k in range(2):
            for copy in p1_copies(r, k):
                copy.start()

    def start_p2(r):
        for k in range(2):
            for copy in p1_copies(r, k):
                copy.wait_recv()
            p2_copy(r, k).start()

    def start_p3(r):
        for k in range(2):
            G, Sd, R = halo[r][k]
            p2_copy(r, k).wait_recv()
            for d in (2, 1, 3, 0):
                t = patch_of(k, first[k], (second[k] + d) % 4, ci)
                at = [spots(k, nbr_ref[j, t]) for j in range(4)]
                north = G[at[0][2], at[0][0], 1]
                south = G[at[1][2], at[1][0], 0]
                if d == 0:
                    R[second[k], 0] = north
                    R[second[k], 1] = south
                else:
                    Sd[d, 0] = north
                    Sd[d, 1] = south
                for v in range(GROUP_ROWS[k] // 16):
                    rows = pl.ds(v * 16, 16)
                    west = G[at[2][2], at[2][0], 2, rows].astype(F32)
                    east = G[at[3][2], at[3][0], 2, rows].astype(F32)
                    mixed = jnp.where(even, east, west).astype(BF16)
                    if d == 0:
                        R[second[k], 2, rows] = mixed
                    else:
                        Sd[d, 2, rows] = mixed
                if d:
                    p3_copy(r, k, d).start()

    def finish_halo(r, T):
        for k in range(2):
            R = halo[r][k][2]
            for d in (2, 1, 3):
                p3_copy(r, k, d).wait_recv()
            at = [spots(k, nbr_ref[j, p])[1] for j in range(4)]
            for v in range(*GROUP_VARS[k]):
                rows = pl.ds((v - GROUP_VARS[k][0]) * 16, 16)
                T[v, :, pl.ds(0, LANES)] = R[at[0], 0, rows].astype(F32)[:SHARE]
                T[v, :, pl.ds(LANES + COLS, LANES)] = R[at[1], 1, rows].astype(F32)[:SHARE]
                west = pltpu.roll(R[at[2], 2, rows].astype(F32), 1, 1)
                east = pltpu.roll(R[at[3], 2, rows].astype(F32), LANES - 1, 1)
                CB[v] = jnp.where(even, west, east)[:SHARE]

    lane = lax.broadcasted_iota(jnp.int32, (SHARE, LANES), 1)

    def strip_mask(x):
        return (lane == 2 * x) | (lane == (2 * x + LANES - 1) % LANES)

    def first_edges():
        def step(x, acc):
            mask = strip_mask(x)
            here = pl.ds(pl.multiple_of((x + 1) * LANES, LANES), LANES)
            return tuple(
                jnp.where(mask, pltpu.roll(S[v, :, here], 2 * x, 1), acc[v]) for v in range(VARS)
            )

        zero = jnp.zeros((SHARE, LANES), F32)
        acc = lax.fori_loop(0, PX, step, (zero,) * VARS)
        for v in range(VARS):
            put_edge(0, 0, v, S[v, :, pl.ds(LANES, LANES)])
            put_edge(0, 1, v, S[v, :, pl.ds(COLS, LANES)])
            put_edge(0, 2, v, acc[v])

    def substep(T, N, r):
        def step(x, acc):
            here = pl.ds(pl.multiple_of((x + 1) * LANES, LANES), LANES)
            above = pl.ds(pl.multiple_of(x * LANES, LANES), LANES)
            below = pl.ds(pl.multiple_of((x + 2) * LANES, LANES), LANES)
            flat = pl.ds(pl.multiple_of(x * LANES, LANES), LANES)
            hx = 0.5 * CX[:, flat]
            hy = 0.5 * CY[:, flat]
            cn, cs, cw, ce = KAPPA + hx, KAPPA - hx, KAPPA + hy, KAPPA - hy
            mask = strip_mask(x)
            new_acc = []
            for v in range(VARS):
                c = T[v, :, here]
                edge = pltpu.roll(CB[v], (LANES - 2 * x) % LANES, 1)
                w = jnp.where(lane == 0, edge, pltpu.roll(c, 1, 1))
                e = jnp.where(lane == LANES - 1, edge, pltpu.roll(c, LANES - 1, 1))
                new = (
                    (1.0 - 4.0 * KAPPA) * c
                    + (cn * T[v, :, above] + cs * T[v, :, below])
                    + (cw * w + ce * e)
                )
                N[v, :, here] = new
                if r is not None:
                    new_acc.append(jnp.where(mask, pltpu.roll(new, 2 * x, 1), acc[v]))
            return tuple(new_acc)

        zero = jnp.zeros((SHARE, LANES), F32)
        acc = lax.fori_loop(0, PX, step, (zero,) * VARS if r is not None else ())
        if r is not None:
            for v in range(VARS):
                put_edge(r, 0, v, N[v, :, pl.ds(LANES, LANES)])
                put_edge(r, 1, v, N[v, :, pl.ds(COLS, LANES)])
                put_edge(r, 2, v, acc[v])

    def prepare():
        j = lax.broadcasted_iota(jnp.int32, (4 * ROWS, 1), 0)
        grp = (j >= ROWS).astype(jnp.int32) + (j >= 2 * ROWS).astype(jnp.int32) + (j >= 3 * ROWS).astype(jnp.int32)
        rest = j - grp * ROWS
        var, lev = rest >> 4, rest & 15
        state_row = var * LEV + grp * SHARE + lev
        surf_row = jnp.where(var < SSHARE, VARS * LEV + grp * SSHARE + var, -1)
        source = jnp.where(lev < SHARE, state_row, surf_row)
        pick = (source == lax.broadcasted_iota(jnp.int32, (4 * ROWS, FEAT), 1)).astype(F32).astype(BF16)
        placed = jnp.dot(pick, w_in[...], preferred_element_type=F32)
        W1[...] = placed.T.astype(BF16)
        source = jnp.where(lev < SHARE, state_row, -1)
        pick = (source == lax.broadcasted_iota(jnp.int32, (4 * ROWS, OUTF), 1)).astype(F32).astype(BF16)
        W2[...] = jnp.dot(pick, w_out[...], preferred_element_type=F32).astype(BF16)
        for i in range(MIDS):
            WM[i] = w_mid[i].astype(F32).T.astype(BF16)
        for i in range(MIDS + 1):
            BB[i] = jnp.broadcast_to(b_hid[i : i + 1, :], (LANES, HID)).T

    def silu(i, pre):
        half = 0.5 * (pre + jnp.concatenate([BB[i]] * (WIDE // LANES), axis=1))
        return (half + half * jnp.tanh(half)).astype(BF16)

    def physics(c):
        whole = pl.ds(c * WIDE, WIDE)
        in_copies(c)[2].wait_recv()
        in_copies(c)[3].wait_recv()
        for copy in in_forwards(c):
            copy.wait_recv()
        hidden = silu(0, jnp.dot(W1[...], X[:, whole], preferred_element_type=F32))
        for i in range(MIDS):
            hidden = silu(i + 1, jnp.dot(WM[i], hidden, preferred_element_type=F32))
        total = jnp.zeros((1, WIDE), F32)
        level = lax.broadcasted_iota(jnp.int32, (16, WIDE), 0)
        for d in range(4):
            tend = jnp.dot(W2[pl.ds(d * ROWS, ROWS)], hidden, preferred_element_type=F32).astype(BF16)
            TO[pl.ds(d * ROWS, ROWS), whole] = tend
            first_var = jnp.where(level < SHARE, tend[:16].astype(F32), 0.0)
            total = total + jnp.sum(first_var, axis=0, keepdims=True)
        total = HEAT_WEIGHT * total
        for i in range(WIDE // LANES):
            HT[pl.ds(c * (WIDE // LANES) + i, 1), :] = total[:, i * LANES : (i + 1) * LANES]
        for copy in out_copies(c):
            copy.start()

    def forward_in(c):
        copies = in_copies(c)
        forwards = in_forwards(c)
        for i in range(2):
            copies[i].wait_recv()
            forwards[i].start()

    def forward_out(c):
        copies = out_copies(c)
        forwards = out_forwards(c)
        for i in range(2):
            copies[i].wait_recv()
            forwards[i].start()

    def heat_copy(d):
        o = (p + d) % 32
        return rcopy(
            PK.at[o], PR.at[p], ht_s.at[d - 1], ht_r.at[d - 1], (g, o)
        )

    def send_heating():
        owner = [owner_ref[p * PX + g * 16 + b] for b in range(16)]
        slot = []
        for b in range(16):
            rank = jnp.int32(0)
            for before in range(b):
                rank = rank + (owner[before] == owner[b]).astype(jnp.int32)
            slot.append(owner[b] * 2 + rank)
        sub = lax.broadcasted_iota(jnp.int32, (8, LANES), 0)
        lines = [jnp.broadcast_to(HT[pl.ds(b, 1), :], (8, LANES)) for b in range(16)]

        def fill(o, carry):
            rows = sub + o * 2
            block = jnp.zeros((8, LANES), F32)
            for b in range(16):
                block = jnp.where(rows == slot[b], lines[b], block)
            PK[o] = block
            return carry

        lax.fori_loop(0, 32, fill, 0)
        PR[p] = PK[p]

        def send(d, carry):
            heat_copy(d).start()
            return carry

        lax.fori_loop(1, 32, send, 0)

    def finish_heating():
        def wait(d, carry):
            heat_copy(d).wait()
            return carry

        lax.fori_loop(1, 32, wait, 0)
        for o in range(32):
            heat_out[pl.ds(o * 2, 2), :] = PR[o, pl.ds(0, 2), :]

    def store(q, c, i):
        off = col0(q, c)
        return pltpu.make_async_copy(
            T1.at[:, :, pl.ds(pl.multiple_of(off + LANES, LANES), WIDE)],
            out.at[:, :, pl.ds(off, WIDE)],
            store_sem.at[c, i],
        )

    def finish(c):
        for copy in out_forwards(c):
            copy.wait_recv()
        out_copies(c)[2].wait_recv()
        out_copies(c)[3].wait_recv()
        whole = pl.ds(c * WIDE, WIDE)
        for i, q in enumerate(order):
            here = pl.ds(pl.multiple_of(col0(q, c) + LANES, LANES), WIDE)
            for v in range(VARS):
                rows = pl.ds(v * 16, 16)
                if i == 3:
                    tend = TO[pl.ds(pl.multiple_of(g * ROWS + v * 16, 16), 16), whole]
                else:
                    tend = TR[q, rows, whole]
                T1[v, :, here] = T1[v, :, here] + PHYS_DT * tend.astype(F32)[:SHARE]
            store(q, c, i).start()

    first_edges()
    start_p1(0)
    prepare()
    forward_in(0)
    start_p2(0)
    for copy in cour:
        copy.wait()
    start_p3(0)
    forward_in(1)
    physics(0)
    finish_halo(0, S)
    substep(S, T1, 1)
    start_p1(1)
    forward_in(2)
    physics(1)
    forward_in(3)
    start_p2(1)
    forward_out(0)
    start_p3(1)
    physics(2)
    finish_halo(1, T1)
    substep(T1, T2, 2)
    start_p1(2)
    forward_out(1)
    physics(3)
    send_heating()
    start_p2(2)
    forward_out(2)
    start_p3(2)
    forward_out(3)
    finish_halo(2, T2)
    substep(T2, T1, None)
    for c in range(CHUNKS):
        finish(c)
    finish_heating()
    for c in range(CHUNKS):
        for copy in in_copies(c) + in_forwards(c) + out_copies(c) + out_forwards(c):
            copy.wait_send()
        for i in range(4):
            store(order[i], c, i).wait()
    for r in range(ROUNDS):
        for k in range(2):
            for copy in p1_copies(r, k):
                copy.wait_send()
            p2_copy(r, k).wait_send()
            for d in (1, 2, 3):
                p3_copy(r, k, d).wait_send()


def on_device(
    state, courant_x, courant_y, surface, w_in, b_hidden, w_mid, w_out, owner_map, neighbours
):
    smem = pl.BlockSpec(memory_space=pltpu.SMEM)
    vmem = pl.BlockSpec(memory_space=pltpu.VMEM)
    anyw = pl.BlockSpec(memory_space=pl.ANY)
    dma = pltpu.SemaphoreType.DMA
    padded = pltpu.VMEM((VARS, SHARE, COLS + 2 * LANES), F32)
    halo_shapes = []
    for lead in ((2, 4, 3), (4, 3), (4, 3)) * ROUNDS:
        for rows in GROUP_ROWS:
            halo_shapes.append(pltpu.VMEM(lead + (rows, LANES), BF16))
    return pl.pallas_call(
        kernel,
        name="couple",
        out_shape=(
            jax.ShapeDtypeStruct((VARS, SHARE, COLS), F32),
            jax.ShapeDtypeStruct((64, LANES), F32),
        ),
        in_specs=[smem, smem, anyw, anyw, anyw] + [vmem] * 5,
        out_specs=(anyw, vmem),
        scratch_shapes=[
            padded, padded, padded,
            pltpu.VMEM((SHARE, COLS), F32), pltpu.VMEM((SHARE, COLS), F32),
            pltpu.VMEM((4, ROWS, QUARTER), BF16),
            pltpu.VMEM((4 * ROWS, QUARTER), BF16),
            pltpu.VMEM((CHUNKS, ROWS, HALF), BF16), pltpu.VMEM((CHUNKS, ROWS, HALF), BF16),
            pltpu.VMEM((4 * ROWS, QUARTER), BF16),
            pltpu.VMEM((4, ROWS, QUARTER), BF16),
            pltpu.VMEM((CHUNKS, ROWS, HALF), BF16), pltpu.VMEM((CHUNKS, ROWS, HALF), BF16),
            pltpu.VMEM((HID, 4 * ROWS), BF16),
            pltpu.VMEM((MIDS, HID, HID), BF16),
            pltpu.VMEM((4 * ROWS, HID), BF16),
            pltpu.VMEM((MIDS + 1, HID, LANES), F32),
            pltpu.VMEM((VARS, SHARE, LANES), F32),
            pltpu.VMEM((16, LANES), F32),
            pltpu.VMEM((32, 8, LANES), F32),
            pltpu.VMEM((32, 8, LANES), F32),
            *halo_shapes,
            dma((CHUNKS, 4)), dma((2,)), dma((CHUNKS, 4)),
            dma((CHUNKS, 4)), dma((CHUNKS, 4)), dma((CHUNKS, 2)), dma((CHUNKS, 2)),
            dma((CHUNKS, 4)), dma((CHUNKS, 4)), dma((CHUNKS, 2)), dma((CHUNKS, 2)),
            dma((ROUNDS, 2, 3)), dma((ROUNDS, 2, 3)), dma((ROUNDS, 2)), dma((ROUNDS, 2)),
            dma((ROUNDS, 2, 3)), dma((ROUNDS, 2, 3)), dma((31,)), dma((31,)),
        ],
        compiler_params=pltpu.CompilerParams(
            collective_id=0, has_side_effects=True, vmem_limit_bytes=56 * 2**20
        ),
    )(
        owner_map.reshape(-1), neighbours.T, state, courant_x, courant_y, surface,
        w_in, b_hidden, w_mid, w_out.T,
    )


def solution(mesh):
    placed = (
        P(None, "grp", "patch"), P("grp", "patch"), P("grp", "patch"), P("grp", "patch"),
        P(), P(), P(), P(), P(), P(),
    )
    return jax.shard_map(
        on_device,
        mesh=mesh,
        in_specs=placed,
        out_specs=(P(None, "grp", "patch"), P("grp", "patch")),
        check_vma=False,
    )
```

time: 367 us -> 104 us (0.28); the launches traced: 361 us -> 103 us
  waiting for transfers between devices: 175 us -> 0 us
  Pallas kernels: 0 us -> 96.6 us
  local copies, waits for them, and re-layouts: 68.4 us -> 5.55 us
  other arithmetic: 60.8 us -> 0 us
  between operations: 30.8 us -> 0.65 us
  starting transfers between devices: 15.3 us -> 0 us
  matrix products: 11 us -> 0 us
    all_gather x6 -> x0, waiting for transfers between devices: 143 us -> none  [the longest x3 86.3 us: on_device(): lax.all_gather(row_edges.astype(jnp.bfloat16), 'patch', axis=0, tiled=True)]
    pallas_call x0 -> x1, Pallas kernels: none -> 96.6 us  [on_device(): pl.pallas_call(kernel, name='couple', out_shape=(jax.ShapeDtypeStruct((VA...]
    all_to_all x3 -> x0, waiting for transfers between devices: 31.3 us -> none  [the longest x1 27.8 us: on_device(): lax.all_to_all(tendency, 'grp', split_axis=2, concat_axis=0, tiled=True)]
    another operation x10 -> x0, other arithmetic: 23.5 us -> none
    another operation x16 -> x0, local copies, waits for them, and re-layouts: 18.1 us -> none  [the longest x6 9.03 us: assemble(): right_band = jnp.swapaxes(take_patch(col_all, east_id)[0], -1, -2)]
    convert_element_type x8 -> x0, other arithmetic: 16 us -> none  [the longest x3 6.84 us: on_device(): lax.all_gather(col_edges.astype(jnp.bfloat16), 'patch', axis=0, tiled=True)]
    reshape x7 -> x0, local copies, waits for them, and re-layouts: 15.9 us -> none  [the longest x1 5.92 us: on_device(): tracer = state.reshape(VARS, level_share, PX, PY)]
    all_to_all x3 -> x0, starting transfers between devices: 14.2 us -> none  [the longest x1 5.24 us: on_device(): lax.all_to_all(packed, 'patch', split_axis=0, concat_axis=0, tiled=True)]
  transfers between devices with their start and end apart: 9 -> 0, of which waited for: 7 -> 0; matrix products, arithmetic and copies ran while one was open for 23% -> 0% of each run, Pallas kernels for 0% -> 0%
where the time goes in v1:
time: 104 us; the launch traced here: 103 us
  Pallas kernels  96.6 us (93%)
  local copies, waits for them, and re-layouts  5.55 us (5%)
    pallas_call x1, Pallas kernels, on_device(): pl.pallas_call(kernel, name='couple', out_shape=(jax.ShapeDtypeStruct((VA...  96.6 us
    unnamed x4, local copies, waits for them, and re-layouts  5.55 us

profile of v1, /device:TPU:0, one launch (start us, length us, event | category | flops | bytes accessed | tf_op | source)
XLA Modules:
  0.0 102.8 jit_solution(8132610428166612518)
XLA Ops:
  0.6 96.6 %couple.1 = (f32[9,15,8192]{2,1,0:T(8,128)}, f32[64,128]{1,0:T(8,128)}) custom-call(s32[2048]{0:T(1024)} %bitcast.4, s32[4,32]{1,0:T(4,128)} %bitcast.5, f32[9,15,8192]{2,1,0:T(8,128)} %state.1, f32[15,8192]{1,0:T(8,128)} %courx.1, f32[15,8192]{1,0:T(8,128)} %coury.1, bf16[4,8192]{1,0:T(4,128)(2,1)} %surf.1, bf16[556,256]{1,0:T(8,128)(2,1)} %w_in.1, ...), custom_call_target="tpu_custom_call" | custom-call | tf_op jit(solution)/shard_map/couple/pallas_call | solution.py:499
  97.2 0.0 copy-start
  97.3 4.9 %copy.14 = f32[9,15,8192]{2,1,0:T(8,128)} copy(f32[9,15,8192]{2,1,0:T(8,128)} %get-tuple-element.4) | data formatting | bytes 8847360
  102.2 0.0 copy-done
  102.2 0.6 copy.15
Async XLA Ops:
  97.2 4.9 %copy-start = (f32[64,128]{1,0:T(8,128)S(1)}, f32[64,128]{1,0:T(8,128)}, u32[]{:S(2)}) copy-start(f32[64,128]{1,0:T(8,128)} %get-tuple-element.5) | copy-start | bytes 98308

commit v2 on v1

--- a/solution.py
+++ b/solution.py
@@ -37,14 +37,15 @@
 
 
 def kernel(
-    owner_ref, nbr_ref, state, courx, coury, surf, w_in, b_hid, w_mid, w_out,
+    owner_ref, nbr_ref, state, courx, coury, surf_in, w_in_in, b_hid_in, w_mid_in, w_out_in,
     out, heat_out,
-    S, T1, T2, CX, CY, F, X, FP, FM, TO, TR, OP, OM,
-    W1, WM, W2, BB, CB, HT, PK, PR,
+    ST, S, T1, CX, CY, HX, HY, surf, w_in, b_hid, w_mid, w_out,
+    F, X, FP, FM, TO, TR, OP, OM,
+    W1, WM, W2, BB, CB, EX, HT, PK, HZ, HZ2, HXX, HC, HR,
     GA0, GB0, SA0, SB0, RA0, RB0, GA1, GB1, SA1, SB1, RA1, RB1, GA2, GB2, SA2, SB2, RA2, RB2,
-    load_sem, cour_sem, store_sem,
+    load_sem, cour_sem, par_sem,
     in_s, in_r, fw_s, fw_r, out_s, out_r, of_s, of_r,
-    p1_s, p1_r, p2_s, p2_r, p3_s, p3_r, ht_s, ht_r,
+    p1_s, p1_r, p2_s, p2_r, p3_s, p3_r, hz_s, hz_r, hx_s, hx_r, hc_s, hc_r,
 ):
     g = lax.axis_index("grp")
     p = lax.axis_index("patch")
@@ -65,43 +66,57 @@
         off = col0(order[i], c)
         return pltpu.make_async_copy(
             state.at[:, :, pl.ds(off, WIDE)],
-            S.at[:, :, pl.ds(pl.multiple_of(off + LANES, LANES), WIDE)],
+            ST.at[:, :, pl.ds(off, WIDE)],
             load_sem.at[c, i],
         )
 
-    for c in range(CHUNKS):
-        for i in range(4):
-            load(c, i).start()
+    params = tuple(
+        pltpu.make_async_copy(src, dst, par_sem.at[i])
+        for i, (src, dst) in enumerate(
+            ((surf_in, surf), (w_in_in, w_in), (b_hid_in, b_hid), (w_mid_in, w_mid), (w_out_in, w_out))
+        )
+    )
     cour = (
         pltpu.make_async_copy(courx, CX, cour_sem.at[0]),
         pltpu.make_async_copy(coury, CY, cour_sem.at[1]),
     )
-    for copy in cour:
-        copy.start()
 
     barrier = pltpu.get_barrier_semaphore()
     for other in (gp, gm, go):
         pl.semaphore_signal(barrier, inc=1, device_id=(other, p), device_id_type=MESH)
-
-    def greet(d, carry):
-        pl.semaphore_signal(barrier, inc=1, device_id=(g, (p + d) % 32), device_id_type=MESH)
-        return carry
-
-    lax.fori_loop(1, 32, greet, 0)
-    pl.semaphore_wait(barrier, 34)
+    for d in (1, 2, 3):
+        pl.semaphore_signal(
+            barrier, inc=1, device_id=(g, zi * 8 + ((xi + d) % 4) * 2 + ci), device_id_type=MESH
+        )
+        pl.semaphore_signal(
+            barrier, inc=1, device_id=(g, ((zi + d) % 4) * 8 + xi * 2 + ci), device_id_type=MESH
+        )
+    pl.semaphore_signal(barrier, inc=1, device_id=(g, p + 1 - 2 * ci), device_id_type=MESH)
+
+    params[0].start()
+    for c in range(CHUNKS):
+        for i in range(4):
+            load(c, i).start()
+    for copy in params[1:] + cour:
+        copy.start()
+    params[0].wait()
+    pl.semaphore_wait(barrier, 10)
 
     def cast(q, c, own):
         off = col0(q, c)
         here = pl.multiple_of(off + LANES, LANES)
         for v in range(VARS):
-            value = S[v, :, pl.ds(here, WIDE)]
+            value = ST[v, :, pl.ds(off, WIDE)]
             if v < SSHARE:
                 extra = surf[v : v + 1, pl.ds(off, WIDE)].astype(F32)
             else:
                 extra = jnp.zeros((1, WIDE), F32)
-            value = jnp.concatenate([value, extra], axis=0).astype(BF16)
-            F[q, pl.ds(v * 16, 16), pl.ds(c * WIDE, WIDE)] = value
-            if own:
+            value = jnp.concatenate([value, extra], axis=0)
+            S[v, :, pl.ds(here, WIDE)] = value
+            value = value.astype(BF16)
+            if not own:
+                F[q, pl.ds(v * 16, 16), pl.ds(c * WIDE, WIDE)] = value
+            else:
                 X[pl.ds(pl.multiple_of(g * ROWS + v * 16, 16), 16), pl.ds(c * WIDE, WIDE)] = value
 
     mine = pl.ds(pl.multiple_of(g * ROWS, 16), ROWS)
@@ -198,9 +213,7 @@
     def put_edge(r, strip, v, value):
         k = 0 if v < SPLIT else 1
         G = halo[r][k][0]
-        G[ci, first[k], strip, pl.ds((v - GROUP_VARS[k][0]) * 16, 16), :] = jnp.concatenate(
-            [value, jnp.zeros((1, LANES), F32)], axis=0
-        ).astype(BF16)
+        G[ci, first[k], strip, pl.ds((v - GROUP_VARS[k][0]) * 16, 16), :] = value
 
     def start_p1(r):
         for k in range(2):
@@ -248,67 +261,63 @@
             at = [spots(k, nbr_ref[j, p])[1] for j in range(4)]
             for v in range(*GROUP_VARS[k]):
                 rows = pl.ds((v - GROUP_VARS[k][0]) * 16, 16)
-                T[v, :, pl.ds(0, LANES)] = R[at[0], 0, rows].astype(F32)[:SHARE]
-                T[v, :, pl.ds(LANES + COLS, LANES)] = R[at[1], 1, rows].astype(F32)[:SHARE]
+                T[v, :, pl.ds(0, LANES)] = R[at[0], 0, rows].astype(F32)
+                T[v, :, pl.ds(LANES + COLS, LANES)] = R[at[1], 1, rows].astype(F32)
                 west = pltpu.roll(R[at[2], 2, rows].astype(F32), 1, 1)
                 east = pltpu.roll(R[at[3], 2, rows].astype(F32), LANES - 1, 1)
-                CB[v] = jnp.where(even, west, east)[:SHARE]
-
-    lane = lax.broadcasted_iota(jnp.int32, (SHARE, LANES), 1)
-
-    def strip_mask(x):
-        return (lane == 2 * x) | (lane == (2 * x + LANES - 1) % LANES)
-
-    def first_edges():
-        def step(x, acc):
-            mask = strip_mask(x)
-            here = pl.ds(pl.multiple_of((x + 1) * LANES, LANES), LANES)
-            return tuple(
-                jnp.where(mask, pltpu.roll(S[v, :, here], 2 * x, 1), acc[v]) for v in range(VARS)
-            )
-
-        zero = jnp.zeros((SHARE, LANES), F32)
-        acc = lax.fori_loop(0, PX, step, (zero,) * VARS)
+                CB[v] = jnp.where(even, west, east).astype(BF16)
+
+    lane = lax.broadcasted_iota(jnp.int32, (16, LANES), 1)
+
+    def edges(T, r):
+        def pick(v, carry):
+            acc = jnp.zeros((16, LANES), BF16)
+            for x in range(PX):
+                mask = (lane == 2 * x) | (lane == (2 * x + LANES - 1) % LANES)
+                tile = T[v, :, pl.ds((x + 1) * LANES, LANES)].astype(BF16)
+                acc = jnp.where(mask, pltpu.roll(tile, 2 * x, 1), acc)
+            EX[v] = acc
+            return carry
+
+        lax.fori_loop(0, VARS, pick, 0)
         for v in range(VARS):
-            put_edge(0, 0, v, S[v, :, pl.ds(LANES, LANES)])
-            put_edge(0, 1, v, S[v, :, pl.ds(COLS, LANES)])
-            put_edge(0, 2, v, acc[v])
-
-    def substep(T, N, r):
-        def step(x, acc):
+            put_edge(r, 0, v, T[v, :, pl.ds(LANES, LANES)].astype(BF16))
+            put_edge(r, 1, v, T[v, :, pl.ds(COLS, LANES)].astype(BF16))
+            put_edge(r, 2, v, EX[v])
+
+    def substep(T, N, part):
+        def step(x, carry):
             here = pl.ds(pl.multiple_of((x + 1) * LANES, LANES), LANES)
             above = pl.ds(pl.multiple_of(x * LANES, LANES), LANES)
             below = pl.ds(pl.multiple_of((x + 2) * LANES, LANES), LANES)
             flat = pl.ds(pl.multiple_of(x * LANES, LANES), LANES)
-            hx = 0.5 * CX[:, flat]
-            hy = 0.5 * CY[:, flat]
+            hx = HX[:, flat]
+            hy = HY[:, flat]
             cn, cs, cw, ce = KAPPA + hx, KAPPA - hx, KAPPA + hy, KAPPA - hy
-            mask = strip_mask(x)
-            new_acc = []
             for v in range(VARS):
                 c = T[v, :, here]
-                edge = pltpu.roll(CB[v], (LANES - 2 * x) % LANES, 1)
+                edge = pltpu.roll(CB[v], (LANES - 2 * x) % LANES, 1).astype(F32)
                 w = jnp.where(lane == 0, edge, pltpu.roll(c, 1, 1))
                 e = jnp.where(lane == LANES - 1, edge, pltpu.roll(c, LANES - 1, 1))
-                new = (
+                N[v, :, here] = (
                     (1.0 - 4.0 * KAPPA) * c
                     + (cn * T[v, :, above] + cs * T[v, :, below])
                     + (cw * w + ce * e)
                 )
-                N[v, :, here] = new
-                if r is not None:
-                    new_acc.append(jnp.where(mask, pltpu.roll(new, 2 * x, 1), acc[v]))
-            return tuple(new_acc)
-
-        zero = jnp.zeros((SHARE, LANES), F32)
-        acc = lax.fori_loop(0, PX, step, (zero,) * VARS if r is not None else ())
-        if r is not None:
-            for v in range(VARS):
-                put_edge(r, 0, v, N[v, :, pl.ds(LANES, LANES)])
-                put_edge(r, 1, v, N[v, :, pl.ds(COLS, LANES)])
-                put_edge(r, 2, v, acc[v])
+            return carry
+
+        lax.fori_loop(part * 16, part * 16 + 16, step, 0, unroll=8)
+
+    def halve():
+        for copy in cour:
+            copy.wait()
+        blank = jnp.zeros((1, COLS), F32)
+        HX[...] = jnp.concatenate([0.5 * CX[...], blank], axis=0)
+        HY[...] = jnp.concatenate([0.5 * CY[...], blank], axis=0)
 
     def prepare():
+        for copy in params[1:]:
+            copy.wait()
         j = lax.broadcasted_iota(jnp.int32, (4 * ROWS, 1), 0)
         grp = (j >= ROWS).astype(jnp.int32) + (j >= 2 * ROWS).astype(jnp.int32) + (j >= 3 * ROWS).astype(jnp.int32)
         rest = j - grp * ROWS
@@ -367,13 +376,25 @@
             copies[i].wait_recv()
             forwards[i].start()
 
-    def heat_copy(d):
-        o = (p + d) % 32
+    def z_copy(d):
+        z = (zi + d) % 4
         return rcopy(
-            PK.at[o], PR.at[p], ht_s.at[d - 1], ht_r.at[d - 1], (g, o)
-        )
-
-    def send_heating():
+            PK.at[pl.ds(pl.multiple_of(z * 16, 16), 16)], HZ.at[zi], hz_s.at[d - 1], hz_r.at[d - 1],
+            (g, z * 8 + xi * 2 + ci),
+        )
+
+    def x_copy(d):
+        x = (xi + d) % 4
+        return rcopy(
+            HZ2.at[x], HXX.at[xi], hx_s.at[d - 1], hx_r.at[d - 1], (g, zi * 8 + x * 2 + ci)
+        )
+
+    def c_copy():
+        return rcopy(
+            HC.at[1 - ci], HR.at[ci], hc_s.at[0], hc_r.at[0], (g, p + 1 - 2 * ci)
+        )
+
+    def heat_z():
         owner = [owner_ref[p * PX + g * 16 + b] for b in range(16)]
         slot = []
         for b in range(16):
@@ -381,100 +402,110 @@
             for before in range(b):
                 rank = rank + (owner[before] == owner[b]).astype(jnp.int32)
             slot.append(owner[b] * 2 + rank)
-        sub = lax.broadcasted_iota(jnp.int32, (8, LANES), 0)
-        lines = [jnp.broadcast_to(HT[pl.ds(b, 1), :], (8, LANES)) for b in range(16)]
-
-        def fill(o, carry):
-            rows = sub + o * 2
-            block = jnp.zeros((8, LANES), F32)
-            for b in range(16):
-                block = jnp.where(rows == slot[b], lines[b], block)
-            PK[o] = block
-            return carry
-
-        lax.fori_loop(0, 32, fill, 0)
-        PR[p] = PK[p]
-
-        def send(d, carry):
-            heat_copy(d).start()
-            return carry
-
-        lax.fori_loop(1, 32, send, 0)
-
-    def finish_heating():
-        def wait(d, carry):
-            heat_copy(d).wait()
-            return carry
-
-        lax.fori_loop(1, 32, wait, 0)
-        for o in range(32):
-            heat_out[pl.ds(o * 2, 2), :] = PR[o, pl.ds(0, 2), :]
-
-    def store(q, c, i):
-        off = col0(q, c)
-        return pltpu.make_async_copy(
-            T1.at[:, :, pl.ds(pl.multiple_of(off + LANES, LANES), WIDE)],
-            out.at[:, :, pl.ds(off, WIDE)],
-            store_sem.at[c, i],
-        )
+        rows = lax.broadcasted_iota(jnp.int32, (64, LANES), 0)
+        table = jnp.zeros((64, LANES), F32)
+        for b in range(16):
+            table = jnp.where(rows == slot[b], jnp.broadcast_to(HT[pl.ds(b, 1), :], (64, LANES)), table)
+        PK[...] = table
+        HZ[zi] = PK[pl.ds(pl.multiple_of(zi * 16, 16), 16), :]
+        for d in (2, 1, 3):
+            z_copy(d).start()
+
+    def heat_x():
+        for d in (2, 1, 3):
+            z_copy(d).wait_recv()
+        for z in range(4):
+            for x in range(4):
+                HZ2[x, pl.ds(z * 4, 4), :] = HZ[z, pl.ds(x * 4, 4), :]
+        HXX[xi] = HZ2[xi]
+        for d in (2, 1, 3):
+            x_copy(d).start()
+
+    def heat_c():
+        for d in (2, 1, 3):
+            x_copy(d).wait_recv()
+        for c in range(2):
+            for z in range(4):
+                for x in range(4):
+                    HC[c, pl.ds(z * 8 + x * 2, 2), :] = HXX[x, pl.ds(z * 4 + c * 2, 2), :]
+        HR[ci] = HC[ci]
+        c_copy().start()
+
+    def heat_end():
+        c_copy().wait_recv()
+        for c in range(2):
+            for z in range(4):
+                for x in range(4):
+                    heat_out[pl.ds(z * 16 + x * 4 + c * 2, 2), :] = HR[c, pl.ds(z * 8 + x * 2, 2), :]
 
     def finish(c):
-        for copy in out_forwards(c):
-            copy.wait_recv()
-        out_copies(c)[2].wait_recv()
-        out_copies(c)[3].wait_recv()
         whole = pl.ds(c * WIDE, WIDE)
-        for i, q in enumerate(order):
+        for i in (3, 2, 1, 0):
+            q = order[i]
+            if i == 2:
+                out_copies(c)[2].wait_recv()
+            elif i == 1:
+                out_copies(c)[3].wait_recv()
+            elif i == 0:
+                for copy in out_forwards(c):
+                    copy.wait_recv()
             here = pl.ds(pl.multiple_of(col0(q, c) + LANES, LANES), WIDE)
             for v in range(VARS):
-                rows = pl.ds(v * 16, 16)
                 if i == 3:
                     tend = TO[pl.ds(pl.multiple_of(g * ROWS + v * 16, 16), 16), whole]
                 else:
-                    tend = TR[q, rows, whole]
-                T1[v, :, here] = T1[v, :, here] + PHYS_DT * tend.astype(F32)[:SHARE]
-            store(q, c, i).start()
-
-    first_edges()
+                    tend = TR[q, pl.ds(v * 16, 16), whole]
+                total = T1[v, :, here] + PHYS_DT * tend.astype(F32)
+                out[v, :, pl.ds(col0(q, c), WIDE)] = total[:SHARE]
+
+    edges(S, 0)
     start_p1(0)
+    halve()
+    forward_in(0)
     prepare()
-    forward_in(0)
     start_p2(0)
-    for copy in cour:
-        copy.wait()
+    forward_in(1)
     start_p3(0)
-    forward_in(1)
     physics(0)
     finish_halo(0, S)
+    substep(S, T1, 0)
     substep(S, T1, 1)
+    forward_in(2)
+    substep(S, T1, 2)
+    substep(S, T1, 3)
+    edges(T1, 1)
     start_p1(1)
-    forward_in(2)
     physics(1)
+    start_p2(1)
     forward_in(3)
-    start_p2(1)
     forward_out(0)
     start_p3(1)
     physics(2)
     finish_halo(1, T1)
-    substep(T1, T2, 2)
+    substep(T1, S, 0)
+    substep(T1, S, 1)
+    forward_out(1)
+    substep(T1, S, 2)
+    substep(T1, S, 3)
+    edges(S, 2)
     start_p1(2)
-    forward_out(1)
     physics(3)
-    send_heating()
+    heat_z()
     start_p2(2)
     forward_out(2)
     start_p3(2)
+    heat_x()
     forward_out(3)
-    finish_halo(2, T2)
-    substep(T2, T1, None)
+    finish_halo(2, S)
+    for part in range(4):
+        substep(S, T1, part)
+    heat_c()
     for c in range(CHUNKS):
         finish(c)
-    finish_heating()
+    heat_end()
     for c in range(CHUNKS):
         for copy in in_copies(c) + in_forwards(c) + out_copies(c) + out_forwards(c):
             copy.wait_send()
-        for i in range(4):
-            store(order[i], c, i).wait()
     for r in range(ROUNDS):
         for k in range(2):
             for copy in p1_copies(r, k):
@@ -482,6 +513,10 @@
             p2_copy(r, k).wait_send()
             for d in (1, 2, 3):
                 p3_copy(r, k, d).wait_send()
+    for d in (1, 2, 3):
+        z_copy(d).wait_send()
+        x_copy(d).wait_send()
+    c_copy().wait_send()
 
 
 def on_device(
@@ -489,9 +524,9 @@
 ):
     smem = pl.BlockSpec(memory_space=pltpu.SMEM)
     vmem = pl.BlockSpec(memory_space=pltpu.VMEM)
-    anyw = pl.BlockSpec(memory_space=pl.ANY)
+    anyw = pl.BlockSpec(memory_space=pltpu.HBM)
     dma = pltpu.SemaphoreType.DMA
-    padded = pltpu.VMEM((VARS, SHARE, COLS + 2 * LANES), F32)
+    padded = pltpu.VMEM((VARS, 16, COLS + 2 * LANES), F32)
     halo_shapes = []
     for lead in ((2, 4, 3), (4, 3), (4, 3)) * ROUNDS:
         for rows in GROUP_ROWS:
@@ -500,14 +535,20 @@
         kernel,
         name="couple",
         out_shape=(
-            jax.ShapeDtypeStruct((VARS, SHARE, COLS), F32),
-            jax.ShapeDtypeStruct((64, LANES), F32),
+            pltpu.VMEM((VARS, SHARE, COLS), F32),
+            pltpu.VMEM((64, LANES), F32),
         ),
-        in_specs=[smem, smem, anyw, anyw, anyw] + [vmem] * 5,
-        out_specs=(anyw, vmem),
+        in_specs=[smem, smem] + [anyw] * 8,
+        out_specs=(vmem, vmem),
         scratch_shapes=[
-            padded, padded, padded,
+            pltpu.VMEM((VARS, SHARE, COLS), F32), padded, padded,
             pltpu.VMEM((SHARE, COLS), F32), pltpu.VMEM((SHARE, COLS), F32),
+            pltpu.VMEM((16, COLS), F32), pltpu.VMEM((16, COLS), F32),
+            pltpu.VMEM((SSHARE, COLS), BF16),
+            pltpu.VMEM((FEAT, HID), BF16),
+            pltpu.VMEM((MIDS + 1, HID), F32),
+            pltpu.VMEM((MIDS, HID, HID), BF16),
+            pltpu.VMEM((OUTF, HID), BF16),
             pltpu.VMEM((4, ROWS, QUARTER), BF16),
             pltpu.VMEM((4 * ROWS, QUARTER), BF16),
             pltpu.VMEM((CHUNKS, ROWS, HALF), BF16), pltpu.VMEM((CHUNKS, ROWS, HALF), BF16),
@@ -518,19 +559,25 @@
             pltpu.VMEM((MIDS, HID, HID), BF16),
             pltpu.VMEM((4 * ROWS, HID), BF16),
             pltpu.VMEM((MIDS + 1, HID, LANES), F32),
-            pltpu.VMEM((VARS, SHARE, LANES), F32),
+            pltpu.VMEM((VARS, 16, LANES), BF16),
+            pltpu.VMEM((VARS, 16, LANES), BF16),
             pltpu.VMEM((16, LANES), F32),
-            pltpu.VMEM((32, 8, LANES), F32),
-            pltpu.VMEM((32, 8, LANES), F32),
+            pltpu.VMEM((64, LANES), F32),
+            pltpu.VMEM((4, 16, LANES), F32),
+            pltpu.VMEM((4, 16, LANES), F32),
+            pltpu.VMEM((4, 16, LANES), F32),
+            pltpu.VMEM((2, 32, LANES), F32),
+            pltpu.VMEM((2, 32, LANES), F32),
             *halo_shapes,
-            dma((CHUNKS, 4)), dma((2,)), dma((CHUNKS, 4)),
+            dma((CHUNKS, 4)), dma((2,)), dma((5,)),
             dma((CHUNKS, 4)), dma((CHUNKS, 4)), dma((CHUNKS, 2)), dma((CHUNKS, 2)),
             dma((CHUNKS, 4)), dma((CHUNKS, 4)), dma((CHUNKS, 2)), dma((CHUNKS, 2)),
             dma((ROUNDS, 2, 3)), dma((ROUNDS, 2, 3)), dma((ROUNDS, 2)), dma((ROUNDS, 2)),
-            dma((ROUNDS, 2, 3)), dma((ROUNDS, 2, 3)), dma((31,)), dma((31,)),
+            dma((ROUNDS, 2, 3)), dma((ROUNDS, 2, 3)),
+            dma((3,)), dma((3,)), dma((3,)), dma((3,)), dma((1,)), dma((1,)),
         ],
         compiler_params=pltpu.CompilerParams(
-            collective_id=0, has_side_effects=True, vmem_limit_bytes=56 * 2**20
+            collective_id=0, has_side_effects=True, vmem_limit_bytes=58 * 2**20
         ),
     )(
         owner_map.reshape(-1), neighbours.T, state, courant_x, courant_y, surface,

time: 104 us -> 76.8 us (0.74)
  Pallas kernels: 96.6 us -> 71.9 us
  local copies, waits for them, and re-layouts: 5.55 us -> 2.8 us
    pallas_call x1, Pallas kernels: 96.6 us -> 71.9 us  [on_device(): pl.pallas_call(kernel, name='couple', out_shape=(pltpu.VMEM((VARS, SHARE,...]
    unnamed x4 -> x2, local copies, waits for them, and re-layouts: 5.55 us -> 2.8 us
where the time goes in v2:
time: 76.8 us; the launch traced here: 75.4 us
  Pallas kernels  71.9 us (94%)
  local copies, waits for them, and re-layouts  2.8 us (4%)
    pallas_call x1, Pallas kernels, on_device(): pl.pallas_call(kernel, name='couple', out_shape=(pltpu.VMEM((VARS, SHARE,...  71.9 us
    unnamed x2, local copies, waits for them, and re-layouts  2.8 us

profile of v2, /device:TPU:0, one launch (start us, length us, event | category | flops | bytes accessed | tf_op | source)
XLA Modules:
  0.0 75.4 jit_solution(2955689297108247527)
XLA Ops:
  0.6 71.9 %couple.1 = (f32[9,15,8192]{2,1,0:T(8,128)S(1)}, f32[64,128]{1,0:T(8,128)S(1)}) custom-call(s32[2048]{0:T(1024)} %bitcast.4, s32[4,32]{1,0:T(4,128)} %bitcast.5, f32[9,15,8192]{2,1,0:T(8,128)} %state.1, f32[15,8192]{1,0:T(8,128)} %courx.1, f32[15,8192]{1,0:T(8,128)} %coury.1, bf16[4,8192]{1,0:T(4,128)(2,1)} %surf_in.1, bf16[556,256]{1,0:T(8,128)(2,1)} %w_in_in.1, ...), custom_call_target="tpu_custom_call" | custom-call | tf_op jit(solution)/shard_map/couple/pallas_call | solution.py:534
  72.6 2.2 %copy.14 = f32[9,15,8192]{2,1,0:T(8,128)} copy(f32[9,15,8192]{2,1,0:T(8,128)S(1)} %get-tuple-element.2) | data formatting | bytes 8847360
  74.7 0.6 copy.15

commit v3 on v2

--- a/solution.py
+++ b/solution.py
@@ -39,7 +39,7 @@
 def kernel(
     owner_ref, nbr_ref, state, courx, coury, surf_in, w_in_in, b_hid_in, w_mid_in, w_out_in,
     out, heat_out,
-    ST, S, T1, CX, CY, HX, HY, surf, w_in, b_hid, w_mid, w_out,
+    ST, S, T1, CX, CY, HX, HY, CK, NS, surf, w_in, b_hid, w_mid, w_out,
     F, X, FP, FM, TO, TR, OP, OM,
     W1, WM, W2, BB, CB, EX, HT, PK, HZ, HZ2, HXX, HC, HR,
     GA0, GB0, SA0, SB0, RA0, RB0, GA1, GB1, SA1, SB1, RA1, RB1, GA2, GB2, SA2, SB2, RA2, RB2,
@@ -100,7 +100,6 @@
     for copy in params[1:] + cour:
         copy.start()
     params[0].wait()
-    pl.semaphore_wait(barrier, 10)
 
     def cast(q, c, own):
         off = col0(q, c)
@@ -156,16 +155,18 @@
             rcopy(OM.at[c], TR.at[gp, :, hi], of_s.at[c, 1], of_r.at[c, 1], (gm, p)),
         )
 
+    def send_in(c):
+        for copy in in_copies(c):
+            copy.start()
+
     for c in range(CHUNKS):
         for i in range(3):
             load(c, i).wait()
             cast(order[i], c, False)
-            copies = in_copies(c)
-            if i == 0:
-                copies[0].start()
-                copies[1].start()
-            else:
-                copies[i + 1].start()
+        if c == 0:
+            pl.semaphore_wait(barrier, 10)
+        if c < 2:
+            send_in(c)
     for c in range(CHUNKS):
         load(c, 3).wait()
         cast(g, c, True)
@@ -253,7 +254,7 @@
                 if d:
                     p3_copy(r, k, d).start()
 
-    def finish_halo(r, T):
+    def finish_halo(r):
         for k in range(2):
             R = halo[r][k][2]
             for d in (2, 1, 3):
@@ -261,25 +262,38 @@
             at = [spots(k, nbr_ref[j, p])[1] for j in range(4)]
             for v in range(*GROUP_VARS[k]):
                 rows = pl.ds((v - GROUP_VARS[k][0]) * 16, 16)
-                T[v, :, pl.ds(0, LANES)] = R[at[0], 0, rows].astype(F32)
-                T[v, :, pl.ds(LANES + COLS, LANES)] = R[at[1], 1, rows].astype(F32)
+                NS[v, 0] = R[at[0], 0, rows]
+                NS[v, 1] = R[at[1], 1, rows]
                 west = pltpu.roll(R[at[2], 2, rows].astype(F32), 1, 1)
                 east = pltpu.roll(R[at[3], 2, rows].astype(F32), LANES - 1, 1)
                 CB[v] = jnp.where(even, west, east).astype(BF16)
 
     lane = lax.broadcasted_iota(jnp.int32, (16, LANES), 1)
 
-    def edges(T, r):
+    def edges(T, r, beside):
         def pick(v, carry):
             acc = jnp.zeros((16, LANES), BF16)
             for x in range(PX):
-                mask = (lane == 2 * x) | (lane == (2 * x + LANES - 1) % LANES)
-                tile = T[v, :, pl.ds((x + 1) * LANES, LANES)].astype(BF16)
-                acc = jnp.where(mask, pltpu.roll(tile, 2 * x, 1), acc)
+                here = pl.ds((x + 1) * LANES, LANES)
+                tile = T[v, :, here]
+                if beside:
+                    flat = pl.ds(x * LANES, LANES)
+                    side = pltpu.roll(CB[v], (LANES - 2 * x) % LANES, 1).astype(F32)
+                    tile = tile + CK[:, flat] * side
+                    if x == 0:
+                        tile = tile + (KAPPA + HX[:, flat]) * NS[v, 0].astype(F32)
+                    if x == PX - 1:
+                        tile = tile + (KAPPA - HX[:, flat]) * NS[v, 1].astype(F32)
+                    T[v, :, here] = tile
+                if r is not None:
+                    mask = (lane == 2 * x) | (lane == (2 * x + LANES - 1) % LANES)
+                    acc = jnp.where(mask, pltpu.roll(tile.astype(BF16), 2 * x, 1), acc)
             EX[v] = acc
             return carry
 
         lax.fori_loop(0, VARS, pick, 0)
+        if r is None:
+            return
         for v in range(VARS):
             put_edge(r, 0, v, T[v, :, pl.ds(LANES, LANES)].astype(BF16))
             put_edge(r, 1, v, T[v, :, pl.ds(COLS, LANES)].astype(BF16))
@@ -293,16 +307,15 @@
             flat = pl.ds(pl.multiple_of(x * LANES, LANES), LANES)
             hx = HX[:, flat]
             hy = HY[:, flat]
-            cn, cs, cw, ce = KAPPA + hx, KAPPA - hx, KAPPA + hy, KAPPA - hy
+            cn, cs = KAPPA + hx, KAPPA - hx
+            cw = jnp.where(lane == 0, 0.0, KAPPA + hy)
+            ce = jnp.where(lane == LANES - 1, 0.0, KAPPA - hy)
             for v in range(VARS):
                 c = T[v, :, here]
-                edge = pltpu.roll(CB[v], (LANES - 2 * x) % LANES, 1).astype(F32)
-                w = jnp.where(lane == 0, edge, pltpu.roll(c, 1, 1))
-                e = jnp.where(lane == LANES - 1, edge, pltpu.roll(c, LANES - 1, 1))
                 N[v, :, here] = (
                     (1.0 - 4.0 * KAPPA) * c
                     + (cn * T[v, :, above] + cs * T[v, :, below])
-                    + (cw * w + ce * e)
+                    + (cw * pltpu.roll(c, 1, 1) + ce * pltpu.roll(c, LANES - 1, 1))
                 )
             return carry
 
@@ -313,7 +326,15 @@
             copy.wait()
         blank = jnp.zeros((1, COLS), F32)
         HX[...] = jnp.concatenate([0.5 * CX[...], blank], axis=0)
-        HY[...] = jnp.concatenate([0.5 * CY[...], blank], axis=0)
+        half = jnp.concatenate([0.5 * CY[...], blank], axis=0)
+        HY[...] = half
+        place = lax.broadcasted_iota(jnp.int32, (16, COLS), 1) & (LANES - 1)
+        CK[...] = jnp.where(
+            place == 0, KAPPA + half, jnp.where(place == LANES - 1, KAPPA - half, 0.0)
+        )
+        for T in (S, T1):
+            T[:, :, pl.ds(0, LANES)] = jnp.zeros((VARS, 16, LANES), F32)
+            T[:, :, pl.ds(LANES + COLS, LANES)] = jnp.zeros((VARS, 16, LANES), F32)
 
     def prepare():
         for copy in params[1:]:
@@ -458,48 +479,53 @@
                 total = T1[v, :, here] + PHYS_DT * tend.astype(F32)
                 out[v, :, pl.ds(col0(q, c), WIDE)] = total[:SHARE]
 
-    edges(S, 0)
+    edges(S, 0, False)
     start_p1(0)
+    forward_in(0)
+    send_in(2)
     halve()
-    forward_in(0)
+    start_p2(0)
     prepare()
-    start_p2(0)
     forward_in(1)
     start_p3(0)
-    physics(0)
-    finish_halo(0, S)
+    send_in(3)
     substep(S, T1, 0)
     substep(S, T1, 1)
-    forward_in(2)
+    physics(0)
     substep(S, T1, 2)
     substep(S, T1, 3)
-    edges(T1, 1)
+    finish_halo(0)
+    edges(T1, 1, True)
     start_p1(1)
+    forward_in(2)
+    substep(T1, S, 0)
+    substep(T1, S, 1)
+    start_p2(1)
     physics(1)
-    start_p2(1)
+    start_p3(1)
     forward_in(3)
     forward_out(0)
-    start_p3(1)
-    physics(2)
-    finish_halo(1, T1)
-    substep(T1, S, 0)
-    substep(T1, S, 1)
-    forward_out(1)
     substep(T1, S, 2)
     substep(T1, S, 3)
-    edges(S, 2)
+    finish_halo(1)
+    edges(S, 2, True)
     start_p1(2)
+    physics(2)
+    start_p2(2)
+    forward_out(1)
     physics(3)
+    start_p3(2)
     heat_z()
-    start_p2(2)
+    substep(S, T1, 0)
+    substep(S, T1, 1)
     forward_out(2)
-    start_p3(2)
     heat_x()
+    substep(S, T1, 2)
+    substep(S, T1, 3)
+    heat_c()
+    finish_halo(2)
     forward_out(3)
-    finish_halo(2, S)
-    for part in range(4):
-        substep(S, T1, part)
-    heat_c()
+    edges(T1, None, True)
     for c in range(CHUNKS):
         finish(c)
     heat_end()
@@ -544,6 +570,7 @@
             pltpu.VMEM((VARS, SHARE, COLS), F32), padded, padded,
             pltpu.VMEM((SHARE, COLS), F32), pltpu.VMEM((SHARE, COLS), F32),
             pltpu.VMEM((16, COLS), F32), pltpu.VMEM((16, COLS), F32),
+            pltpu.VMEM((16, COLS), F32), pltpu.VMEM((VARS, 2, 16, LANES), BF16),
             pltpu.VMEM((SSHARE, COLS), BF16),
             pltpu.VMEM((FEAT, HID), BF16),
             pltpu.VMEM((MIDS + 1, HID), F32),

time: 76.8 us -> 65.4 us (0.85); the launches traced: 75.4 us -> 65.3 us
  Pallas kernels: 71.9 us -> 61.8 us
    pallas_call x1, Pallas kernels: 71.9 us -> 61.8 us  [on_device(): pl.pallas_call(kernel, name='couple', out_shape=(pltpu.VMEM((VARS, SHARE,...]
where the time goes in v3:
time: 65.4 us; the launch traced here: 65.3 us
  Pallas kernels  61.8 us (94%)
  local copies, waits for them, and re-layouts  2.8 us (4%)
    pallas_call x1, Pallas kernels, on_device(): pl.pallas_call(kernel, name='couple', out_shape=(pltpu.VMEM((VARS, SHARE,...  61.8 us
    unnamed x2, local copies, waits for them, and re-layouts  2.8 us

profile of v3, /device:TPU:0, one launch (start us, length us, event | category | flops | bytes accessed | tf_op | source)
XLA Modules:
  0.0 65.3 jit_solution(96666168987228270)
XLA Ops:
  0.6 61.8 %couple.1 = (f32[9,15,8192]{2,1,0:T(8,128)S(1)}, f32[64,128]{1,0:T(8,128)S(1)}) custom-call(s32[2048]{0:T(1024)} %bitcast.4, s32[4,32]{1,0:T(4,128)} %bitcast.5, f32[9,15,8192]{2,1,0:T(8,128)} %state.1, f32[15,8192]{1,0:T(8,128)} %courx.1, f32[15,8192]{1,0:T(8,128)} %coury.1, bf16[4,8192]{1,0:T(4,128)(2,1)} %surf_in.1, bf16[556,256]{1,0:T(8,128)(2,1)} %w_in_in.1, ...), custom_call_target="tpu_custom_call" | custom-call | tf_op jit(solution)/shard_map/couple/pallas_call | solution.py:560
  62.5 2.2 %copy.14 = f32[9,15,8192]{2,1,0:T(8,128)} copy(f32[9,15,8192]{2,1,0:T(8,128)S(1)} %get-tuple-element.2) | data formatting | bytes 8847360
  64.6 0.6 copy.15

commit v4 on v3

--- a/solution.py
+++ b/solution.py
@@ -21,6 +21,7 @@
 COLS = PX * LANES
 QUARTER = COLS // 4
 ROWS = VARS * 16
+OROWS = 136
 FEAT = 556
 OUTF = 540
 CHUNKS = 4
@@ -40,7 +41,7 @@
     owner_ref, nbr_ref, state, courx, coury, surf_in, w_in_in, b_hid_in, w_mid_in, w_out_in,
     out, heat_out,
     ST, S, T1, CX, CY, HX, HY, CK, NS, surf, w_in, b_hid, w_mid, w_out,
-    F, X, FP, FM, TO, TR, OP, OM,
+    F, X, FP, FM, TN, TF, RN, RF, OP, OM,
     W1, WM, W2, BB, CB, EX, HT, PK, HZ, HZ2, HXX, HC, HR,
     GA0, GB0, SA0, SB0, RA0, RB0, GA1, GB1, SA1, SB1, RA1, RB1, GA2, GB2, SA2, SB2, RA2, RB2,
     load_sem, cour_sem, par_sem,
@@ -121,7 +122,6 @@
     mine = pl.ds(pl.multiple_of(g * ROWS, 16), ROWS)
     prev_rows = pl.ds(pl.multiple_of(gm * ROWS, 16), ROWS)
     next_rows = pl.ds(pl.multiple_of(gp * ROWS, 16), ROWS)
-    far_rows = pl.ds(pl.multiple_of(go * ROWS, 16), ROWS)
 
     def in_copies(c):
         lo, hi, whole = pl.ds(c * WIDE, HALF), pl.ds(c * WIDE + HALF, HALF), pl.ds(c * WIDE, WIDE)
@@ -140,19 +140,17 @@
         )
 
     def out_copies(c):
-        lo, hi, whole = pl.ds(c * WIDE, HALF), pl.ds(c * WIDE + HALF, HALF), pl.ds(c * WIDE, WIDE)
         return (
-            rcopy(TO.at[far_rows, lo], OP.at[c], out_s.at[c, 0], out_r.at[c, 0], (gp, p)),
-            rcopy(TO.at[far_rows, hi], OM.at[c], out_s.at[c, 1], out_r.at[c, 1], (gm, p)),
-            rcopy(TO.at[next_rows, whole], TR.at[g, :, whole], out_s.at[c, 2], out_r.at[c, 2], (gp, p)),
-            rcopy(TO.at[prev_rows, whole], TR.at[g, :, whole], out_s.at[c, 3], out_r.at[c, 3], (gm, p)),
+            rcopy(TF.at[c, 0], OP.at[c], out_s.at[c, 0], out_r.at[c, 0], (gp, p)),
+            rcopy(TF.at[c, 1], OM.at[c], out_s.at[c, 1], out_r.at[c, 1], (gm, p)),
+            rcopy(TN.at[0, c], RN.at[0, c], out_s.at[c, 2], out_r.at[c, 2], (gp, p)),
+            rcopy(TN.at[1, c], RN.at[1, c], out_s.at[c, 3], out_r.at[c, 3], (gm, p)),
         )
 
     def out_forwards(c):
-        lo, hi = pl.ds(c * WIDE, HALF), pl.ds(c * WIDE + HALF, HALF)
         return (
-            rcopy(OP.at[c], TR.at[gm, :, lo], of_s.at[c, 0], of_r.at[c, 0], (gp, p)),
-            rcopy(OM.at[c], TR.at[gp, :, hi], of_s.at[c, 1], of_r.at[c, 1], (gm, p)),
+            rcopy(OP.at[c], RF.at[0, c], of_s.at[c, 0], of_r.at[c, 0], (gp, p)),
+            rcopy(OM.at[c], RF.at[1, c], of_s.at[c, 1], of_r.at[c, 1], (gm, p)),
         )
 
     def send_in(c):
@@ -349,9 +347,18 @@
         pick = (source == lax.broadcasted_iota(jnp.int32, (4 * ROWS, FEAT), 1)).astype(F32).astype(BF16)
         placed = jnp.dot(pick, w_in[...], preferred_element_type=F32)
         W1[...] = placed.T.astype(BF16)
-        source = jnp.where(lev < SHARE, state_row, -1)
-        pick = (source == lax.broadcasted_iota(jnp.int32, (4 * ROWS, OUTF), 1)).astype(F32).astype(BF16)
-        W2[...] = jnp.dot(pick, w_out[...], preferred_element_type=F32).astype(BF16)
+        j = lax.broadcasted_iota(jnp.int32, (4 * OROWS, 1), 0)
+        grp = (j >= OROWS).astype(jnp.int32) + (j >= 2 * OROWS).astype(jnp.int32) + (j >= 3 * OROWS).astype(jnp.int32)
+        rest = j - grp * OROWS
+        var, lev = rest >> 4, rest & 15
+        last = (VARS - 1) * LEV + grp * SHARE
+        main_row = jnp.where(lev < SHARE, var * LEV + grp * SHARE + lev, last + var)
+        tail_row = jnp.where(rest < OROWS - 1, last + rest - 120, -1)
+        source = jnp.where(rest < 128, main_row, tail_row)
+        pick = (source == lax.broadcasted_iota(jnp.int32, (4 * OROWS, OUTF), 1)).astype(F32).astype(BF16)
+        placed = jnp.dot(pick, w_out[...], preferred_element_type=F32)
+        for d in range(4):
+            W2[d] = placed[d * OROWS : (d + 1) * OROWS].astype(BF16)
         for i in range(MIDS):
             WM[i] = w_mid[i].astype(F32).T.astype(BF16)
         for i in range(MIDS + 1):
@@ -372,10 +379,20 @@
             hidden = silu(i + 1, jnp.dot(WM[i], hidden, preferred_element_type=F32))
         total = jnp.zeros((1, WIDE), F32)
         level = lax.broadcasted_iota(jnp.int32, (16, WIDE), 0)
-        for d in range(4):
-            tend = jnp.dot(W2[pl.ds(d * ROWS, ROWS)], hidden, preferred_element_type=F32).astype(BF16)
-            TO[pl.ds(d * ROWS, ROWS), whole] = tend
-            first_var = jnp.where(level < SHARE, tend[:16].astype(F32), 0.0)
+        def pack(ref, tend):
+            n = tend.shape[1] // 2
+            ref[pl.ds(0, 128), :] = tend[:128, :n].astype(BF16)
+            ref[pl.ds(128, 128), :] = tend[:128, n:].astype(BF16)
+            ref[pl.ds(256, 16), :] = jnp.concatenate([tend[128:, :n], tend[128:, n:]], axis=0).astype(BF16)
+
+        for i, d in enumerate((gp, gm, g, go)):
+            tend = jnp.dot(W2[d], hidden, preferred_element_type=F32)
+            if i < 3:
+                pack(TN.at[i, c], tend)
+            else:
+                pack(TF.at[c, 0], tend[:, :HALF])
+                pack(TF.at[c, 1], tend[:, HALF:])
+            first_var = jnp.where(level < SHARE, tend[:16].astype(BF16).astype(F32), 0.0)
             total = total + jnp.sum(first_var, axis=0, keepdims=True)
         total = HEAT_WEIGHT * total
         for i in range(WIDE // LANES):
@@ -459,25 +476,30 @@
                 for x in range(4):
                     heat_out[pl.ds(z * 16 + x * 4 + c * 2, 2), :] = HR[c, pl.ds(z * 8 + x * 2, 2), :]
 
+    def add(ref, off, wide):
+        n = wide // 2
+        tail = ref[pl.ds(256, 16), :].astype(F32)
+        for i in range(2):
+            flat = pl.ds(pl.multiple_of(off + i * n, LANES), n)
+            here = pl.ds(pl.multiple_of(off + i * n + LANES, LANES), n)
+            extra = []
+            for v in range(VARS - 1):
+                tend = ref[pl.ds(i * 128 + v * 16, 16), :].astype(F32)
+                extra.append(tend[SHARE:])
+                total = T1[v, :, here] + PHYS_DT * tend
+                out[v, :, flat] = total[:SHARE]
+            tend = jnp.concatenate(extra + [tail[i * 8 : i * 8 + 7]], axis=0)
+            out[VARS - 1, :, flat] = T1[VARS - 1, :, here][:SHARE] + PHYS_DT * tend
+
     def finish(c):
-        whole = pl.ds(c * WIDE, WIDE)
-        for i in (3, 2, 1, 0):
-            q = order[i]
-            if i == 2:
-                out_copies(c)[2].wait_recv()
-            elif i == 1:
-                out_copies(c)[3].wait_recv()
-            elif i == 0:
-                for copy in out_forwards(c):
-                    copy.wait_recv()
-            here = pl.ds(pl.multiple_of(col0(q, c) + LANES, LANES), WIDE)
-            for v in range(VARS):
-                if i == 3:
-                    tend = TO[pl.ds(pl.multiple_of(g * ROWS + v * 16, 16), 16), whole]
-                else:
-                    tend = TR[q, pl.ds(v * 16, 16), whole]
-                total = T1[v, :, here] + PHYS_DT * tend.astype(F32)
-                out[v, :, pl.ds(col0(q, c), WIDE)] = total[:SHARE]
+        add(TN.at[2, c], col0(g, c), WIDE)
+        out_copies(c)[2].wait_recv()
+        add(RN.at[0, c], col0(gm, c), WIDE)
+        out_copies(c)[3].wait_recv()
+        add(RN.at[1, c], col0(gp, c), WIDE)
+        for i in range(2):
+            out_forwards(c)[i].wait_recv()
+            add(RF.at[i, c], pl.multiple_of(col0(go, c) + i * HALF, LANES), HALF)
 
     edges(S, 0, False)
     start_p1(0)
@@ -512,9 +534,9 @@
     start_p1(2)
     physics(2)
     start_p2(2)
-    forward_out(1)
     physics(3)
     start_p3(2)
+    forward_out(1)
     heat_z()
     substep(S, T1, 0)
     substep(S, T1, 1)
@@ -523,8 +545,8 @@
     substep(S, T1, 2)
     substep(S, T1, 3)
     heat_c()
+    forward_out(3)
     finish_halo(2)
-    forward_out(3)
     edges(T1, None, True)
     for c in range(CHUNKS):
         finish(c)
@@ -545,26 +567,36 @@
     c_copy().wait_send()
 
 
+def write_out(new, heat, new_hbm, heat_hbm, sems):
+    copies = [pltpu.make_async_copy(new.at[v], new_hbm.at[v], sems.at[v]) for v in range(VARS)]
+    copies.append(pltpu.make_async_copy(heat, heat_hbm, sems.at[VARS]))
+    for copy in copies:
+        copy.start()
+    for copy in copies:
+        copy.wait()
+
+
 def on_device(
     state, courant_x, courant_y, surface, w_in, b_hidden, w_mid, w_out, owner_map, neighbours
 ):
     smem = pl.BlockSpec(memory_space=pltpu.SMEM)
     vmem = pl.BlockSpec(memory_space=pltpu.VMEM)
-    anyw = pl.BlockSpec(memory_space=pltpu.HBM)
+    hbm = pl.BlockSpec(memory_space=pltpu.HBM)
+    anyw = pl.BlockSpec(memory_space=pl.ANY)
     dma = pltpu.SemaphoreType.DMA
     padded = pltpu.VMEM((VARS, 16, COLS + 2 * LANES), F32)
     halo_shapes = []
     for lead in ((2, 4, 3), (4, 3), (4, 3)) * ROUNDS:
         for rows in GROUP_ROWS:
             halo_shapes.append(pltpu.VMEM(lead + (rows, LANES), BF16))
-    return pl.pallas_call(
+    new, heat = pl.pallas_call(
         kernel,
         name="couple",
         out_shape=(
             pltpu.VMEM((VARS, SHARE, COLS), F32),
             pltpu.VMEM((64, LANES), F32),
         ),
-        in_specs=[smem, smem] + [anyw] * 8,
+        in_specs=[smem, smem] + [hbm] * 8,
         out_specs=(vmem, vmem),
         scratch_shapes=[
             pltpu.VMEM((VARS, SHARE, COLS), F32), padded, padded,
@@ -579,12 +611,15 @@
             pltpu.VMEM((4, ROWS, QUARTER), BF16),
             pltpu.VMEM((4 * ROWS, QUARTER), BF16),
             pltpu.VMEM((CHUNKS, ROWS, HALF), BF16), pltpu.VMEM((CHUNKS, ROWS, HALF), BF16),
-            pltpu.VMEM((4 * ROWS, QUARTER), BF16),
-            pltpu.VMEM((4, ROWS, QUARTER), BF16),
-            pltpu.VMEM((CHUNKS, ROWS, HALF), BF16), pltpu.VMEM((CHUNKS, ROWS, HALF), BF16),
+            pltpu.VMEM((3, CHUNKS, 2 * OROWS, WIDE // 2), BF16),
+            pltpu.VMEM((CHUNKS, 2, 2 * OROWS, HALF // 2), BF16),
+            pltpu.VMEM((2, CHUNKS, 2 * OROWS, WIDE // 2), BF16),
+            pltpu.VMEM((2, CHUNKS, 2 * OROWS, HALF // 2), BF16),
+            pltpu.VMEM((CHUNKS, 2 * OROWS, HALF // 2), BF16),
+            pltpu.VMEM((CHUNKS, 2 * OROWS, HALF // 2), BF16),
             pltpu.VMEM((HID, 4 * ROWS), BF16),
             pltpu.VMEM((MIDS, HID, HID), BF16),
-            pltpu.VMEM((4 * ROWS, HID), BF16),
+            pltpu.VMEM((4, OROWS, HID), BF16),
             pltpu.VMEM((MIDS + 1, HID, LANES), F32),
             pltpu.VMEM((VARS, 16, LANES), BF16),
             pltpu.VMEM((VARS, 16, LANES), BF16),
@@ -610,6 +645,21 @@
         owner_map.reshape(-1), neighbours.T, state, courant_x, courant_y, surface,
         w_in, b_hidden, w_mid, w_out.T,
     )
+    return pl.pallas_call(
+        write_out,
+        name="write_out",
+        out_shape=(
+            jax.ShapeDtypeStruct((VARS, SHARE, COLS), F32),
+            jax.ShapeDtypeStruct((64, LANES), F32),
+        ),
+        in_specs=[anyw, anyw],
+        out_specs=(hbm, hbm),
+        scratch_shapes=[dma((VARS + 1,))],
+        compiler_params=pltpu.CompilerParams(vmem_limit_bytes=2**20),
+    )(
+        pltpu.with_memory_space_constraint(new, pltpu.VMEM),
+        pltpu.with_memory_space_constraint(heat, pltpu.VMEM),
+    )
 
 
 def solution(mesh):

time: 65.4 us -> 64.6 us (0.988)
  local copies, waits for them, and re-layouts: 2.8 us -> 0 us
  Pallas kernels: 61.8 us -> 63.8 us
    unnamed x2 -> x0, local copies, waits for them, and re-layouts: 2.8 us -> none
    pallas_call x0 -> x1, Pallas kernels: none -> 2.26 us  [on_device(): pl.pallas_call(write_out, name='write_out', out_shape=(jax.ShapeDtypeStru...]
where the time goes in v4:
time: 64.6 us; the launch traced here: 64.5 us
  Pallas kernels  63.8 us (99%)
    pallas_call x1, Pallas kernels, on_device(): pl.pallas_call(kernel, name='couple', out_shape=(pltpu.VMEM((VARS, SHARE,...  61.6 us
    pallas_call x1, Pallas kernels, on_device(): pl.pallas_call(write_out, name='write_out', out_shape=(jax.ShapeDtypeStru...  2.26 us

profile of v4, /device:TPU:0, one launch (start us, length us, event | category | flops | bytes accessed | tf_op | source)
XLA Modules:
  0.0 64.5 jit_solution(16693040760630493736)
XLA Ops:
  0.6 61.6 %couple.1 = (f32[9,15,8192]{2,1,0:T(8,128)S(1)}, f32[64,128]{1,0:T(8,128)S(1)}) custom-call(s32[2048]{0:T(1024)} %bitcast.4, s32[4,32]{1,0:T(4,128)} %bitcast.5, f32[9,15,8192]{2,1,0:T(8,128)} %state.1, f32[15,8192]{1,0:T(8,128)} %courx.1, f32[15,8192]{1,0:T(8,128)} %coury.1, bf16[4,8192]{1,0:T(4,128)(2,1)} %surf_in.1, bf16[556,256]{1,0:T(8,128)(2,1)} %w_in_in.1, ...), custom_call_target="tpu_custom_call" | custom-call | tf_op jit(solution)/shard_map/couple/pallas_call | solution.py:592
  62.2 2.3 %write_out.1 = (f32[9,15,8192]{2,1,0:T(8,128)}, f32[64,128]{1,0:T(8,128)}) custom-call(f32[9,15,8192]{2,1,0:T(8,128)S(1)} %get-tuple-element.4.new, f32[64,128]{1,0:T(8,128)S(1)} %get-tuple-element.5.heat), custom_call_target="tpu_custom_call" | custom-call | tf_op jit(solution)/shard_map/write_out/pallas_call | solution.py:648

commit v5 on v4

--- a/solution.py
+++ b/solution.py
@@ -513,12 +513,12 @@
     send_in(3)
     substep(S, T1, 0)
     substep(S, T1, 1)
-    physics(0)
     substep(S, T1, 2)
     substep(S, T1, 3)
     finish_halo(0)
     edges(T1, 1, True)
     start_p1(1)
+    physics(0)
     forward_in(2)
     substep(T1, S, 0)
     substep(T1, S, 1)

time: 64.6 us -> 63.9 us (0.989)
  Pallas kernels: 63.8 us -> 63.1 us
    pallas_call x1, Pallas kernels: 61.6 us -> 60.8 us  [on_device(): pl.pallas_call(kernel, name='couple', out_shape=(pltpu.VMEM((VARS, SHARE,...]
where the time goes in v5:
time: 63.9 us; the launch traced here: 63.7 us
  Pallas kernels  63.1 us (99%)
  between operations  0.64 us (1%)
    pallas_call x1, Pallas kernels, on_device(): pl.pallas_call(kernel, name='couple', out_shape=(pltpu.VMEM((VARS, SHARE,...  60.8 us
    pallas_call x1, Pallas kernels, on_device(): pl.pallas_call(write_out, name='write_out', out_shape=(jax.ShapeDtypeStru...  2.26 us

profile of v5, /device:TPU:0, one launch (start us, length us, event | category | flops | bytes accessed | tf_op | source)
XLA Modules:
  0.0 63.7 jit_solution(6722703641087043925)
XLA Ops:
  0.6 60.8 %couple.1 = (f32[9,15,8192]{2,1,0:T(8,128)S(1)}, f32[64,128]{1,0:T(8,128)S(1)}) custom-call(s32[2048]{0:T(1024)} %bitcast.4, s32[4,32]{1,0:T(4,128)} %bitcast.5, f32[9,15,8192]{2,1,0:T(8,128)} %state.1, f32[15,8192]{1,0:T(8,128)} %courx.1, f32[15,8192]{1,0:T(8,128)} %coury.1, bf16[4,8192]{1,0:T(4,128)(2,1)} %surf_in.1, bf16[556,256]{1,0:T(8,128)(2,1)} %w_in_in.1, ...), custom_call_target="tpu_custom_call" | custom-call | tf_op jit(solution)/shard_map/couple/pallas_call | solution.py:592
  61.5 2.3 %write_out.1 = (f32[9,15,8192]{2,1,0:T(8,128)}, f32[64,128]{1,0:T(8,128)}) custom-call(f32[9,15,8192]{2,1,0:T(8,128)S(1)} %get-tuple-element.4.new, f32[64,128]{1,0:T(8,128)S(1)} %get-tuple-element.5.heat), custom_call_target="tpu_custom_call" | custom-call | tf_op jit(solution)/shard_map/write_out/pallas_call | solution.py:648
